TPU v7x, 32 devices: a whole 2x2x4 slice. The times are simulated.
32 devices in a mesh: section: 2 (over x), dp: 16 (over z, y, core).
Axes of the slice: x: 2, y: 2, z: 4, core: 2. Of those that a mesh axis runs over, the one named last changes fastest.
Arguments:
- embeds: bfloat16 [2, 32, 1024, 512], P('section', 'dp'), may hold values from -6 to 6
- cotangent: bfloat16 [2, 32, 1024, 512], P('section', 'dp'), may hold values from -6 to 6
- pair_ids: int32 [32], P('dp'), may hold values from 0 to 15
- seq_lengths: int32 [2, 32], P(None, 'dp'), may hold values from 512 to 1024, as said below
- alive_count: int32 [16], P('dp'), may hold values from 1 to 2, as said below
- self_proj: bfloat16 [2, 3, 512, 512], P('section'), may hold values from -0.25 to 0.25
- self_out: bfloat16 [2, 512, 512], P('section'), may hold values from -2 to 2
- self_bias: float32 [2, 3, 512], P('section'), may hold values from -1.75 to 1.75
- ffn_in: bfloat16 [2, 512, 2048], P('section'), may hold values from -0.25 to 0.25
- ffn_in_bias: float32 [2, 2048], P('section'), may hold values from -1.75 to 1.75
- ffn_out: bfloat16 [2, 2048, 512], P('section'), may hold values from -0.125 to 0.125
- ffn_out_bias: float32 [2, 512], P('section'), may hold values from -1.75 to 1.75
- norm_gain: float32 [2, 2, 512], P('section'), may hold values from 0.5 to 1.5
- norm_bias: float32 [2, 2, 512], P('section'), may hold values from -1.75 to 1.75
- cross_proj: bfloat16 [3, 512, 512], replicated, may hold values from -0.25 to 0.25
- cross_out: bfloat16 [512, 512], replicated, may hold values from -2 to 2
- cross_bias: float32 [3, 512], replicated, may hold values from -1.75 to 1.75
- cross_norm_gain: float32 [512], replicated, may hold values from 0.5 to 1.5
- cross_norm_bias: float32 [512], replicated, may hold values from -1.75 to 1.75
- pair_embed: float32 [16, 512], replicated, may hold values from -3 to 3
Outputs:
- layer_out: bfloat16 [2, 32, 1024, 512], P('section', 'dp')
- embeds_grad: float32 [2, 32, 1024, 512], P('section', 'dp')
- self_proj_grad: float32 [2, 3, 512, 512], P('section')
- self_out_grad: float32 [2, 512, 512], P('section')
- self_bias_grad: float32 [2, 3, 512], P('section')
- ffn_in_grad: float32 [2, 512, 2048], P('section')
- ffn_in_bias_grad: float32 [2, 2048], P('section')
- ffn_out_grad: float32 [2, 2048, 512], P('section')
- ffn_out_bias_grad: float32 [2, 512], P('section')
- norm_gain_grad: float32 [2, 2, 512], P('section')
- norm_bias_grad: float32 [2, 2, 512], P('section')
- cross_proj_grad: float32 [3, 512, 512], replicated
- cross_out_grad: float32 [512, 512], replicated
- cross_bias_grad: float32 [3, 512], replicated
- cross_norm_gain_grad: float32 [512], replicated
- cross_norm_bias_grad: float32 [512], replicated
- pair_embed_grad: float32 [16, 512], replicated
Inputs may be any that keep to these rules, and one draw needn't show every extreme that they name: `seq_lengths`: in each row some sequence has exactly 1024 tokens. `alive_count`: sequence slots of a device at or past its count are padding; some device is full.
All inputs are finite; a program needn't handle non-finite values.
Results may differ from a plain program's by a relative error of at most 0.014.
Values may be sent and summed in bfloat16 or wider, within the bound.
A program may use at most 320 MiB of HBM per device.

v0:
```python
import jax
import jax.numpy as jnp
from jax import lax
from jax.sharding import PartitionSpec as P

HEADS = 8


EPSILON = 1e-05
MASKED = -1000000000.0


def from_behind(value, axis, steps):
    count = lax.axis_size(axis)
    leading, last = (max(0, -steps), min(count, count - steps))
    return lax.ppermute(value, axis, [(source, source + steps) for source in range(leading, last)])


def matmul(left, right):
    return jnp.dot(left, right, preferred_element_type=jnp.float32)


def bias_sum(grad_low):
    return jnp.sum(grad_low.astype(jnp.float32), axis=0)


def layer_norm(value, gain, offset):
    centre = jnp.mean(value, -1, keepdims=True)
    centred = value - centre
    spread = jnp.mean(centred * centred, -1, keepdims=True)
    return centred * lax.rsqrt(spread + EPSILON) * gain + offset


def norm_back(value, gain, offset, grad):
    unused, puller = jax.vjp(layer_norm, value, gain, offset)
    return puller(grad)


def smooth(value):
    return jax.nn.gelu(value, approximate=False)


def split_heads(value):
    return value.reshape(value.shape[0], HEADS, value.shape[1] // HEADS)


def join_heads(value):
    return value.reshape(value.shape[0], value.shape[1] * value.shape[2]).astype(jnp.bfloat16)


def scale_of(queries):
    return (queries.shape[1] // HEADS) ** (-0.5)


def key_mask(row_count, length):
    positions = jnp.arange(row_count)
    return jnp.broadcast_to(positions[None, :] < length, (row_count, row_count))


def causal_mask(row_count, length):
    positions = jnp.arange(row_count)
    return (positions[None, :] <= positions[:, None]) & (positions[None, :] < length)


def mix_forward(queries, key_rows, values, allowed):
    scores = jnp.einsum(
        "qhd,khd->hqk",
        split_heads(queries),
        split_heads(key_rows),
        preferred_element_type=jnp.float32,
    ) * scale_of(queries)
    scores = jnp.where(allowed[None], scores, MASKED)
    attn_probs = jax.nn.softmax(scores, axis=-1)
    mixed_rows = jnp.einsum(
        "hqk,khd->qhd",
        attn_probs.astype(jnp.bfloat16),
        split_heads(values),
        preferred_element_type=jnp.float32,
    )
    return (join_heads(mixed_rows), attn_probs)


def mix_back(queries, key_rows, values, attn_probs, grad_mixed):
    scaling = scale_of(queries)
    grad_heads = split_heads(grad_mixed)
    grad_values = jnp.einsum(
        "hqk,qhd->khd",
        attn_probs.astype(jnp.bfloat16),
        grad_heads,
        preferred_element_type=jnp.float32,
    )
    grad_probs = jnp.einsum(
        "qhd,khd->hqk", grad_heads, split_heads(values), preferred_element_type=jnp.float32
    )
    grad_scores = attn_probs * (grad_probs - jnp.sum(grad_probs * attn_probs, -1, keepdims=True))
    grad_scores = grad_scores.astype(jnp.bfloat16)
    grad_queries = (
        jnp.einsum(
            "hqk,khd->qhd", grad_scores, split_heads(key_rows), preferred_element_type=jnp.float32
        )
        * scaling
    )
    grad_keys = (
        jnp.einsum(
            "hqk,qhd->khd", grad_scores, split_heads(queries), preferred_element_type=jnp.float32
        )
        * scaling
    )
    return (join_heads(grad_queries), join_heads(grad_keys), join_heads(grad_values))


def self_project(inputs_low, projection, bias_rows):
    queries = (matmul(inputs_low, projection[0]) + bias_rows[0]).astype(jnp.bfloat16)
    key_rows = matmul(inputs_low, projection[1]).astype(jnp.bfloat16)
    values = (matmul(inputs_low, projection[2]) + bias_rows[1]).astype(jnp.bfloat16)
    return (queries, key_rows, values)


def output_back(mixed_rows, out_w, grad):
    grad_low = grad.astype(jnp.bfloat16)
    return (
        matmul(mixed_rows.T, grad_low),
        bias_sum(grad_low),
        matmul(grad_low, out_w.T).astype(jnp.bfloat16),
    )


def self_back(
    inputs_low, projection, out_w, queries, key_rows, values, attn_probs, mixed_rows, grad
):
    d_out, d_bias_out, grad_mixed = output_back(mixed_rows, out_w, grad)
    grad_q, grad_k, grad_v = mix_back(queries, key_rows, values, attn_probs, grad_mixed)
    d_proj = jnp.stack(
        [matmul(inputs_low.T, grad_q), matmul(inputs_low.T, grad_k), matmul(inputs_low.T, grad_v)]
    )
    d_bias = jnp.stack([bias_sum(grad_q), bias_sum(grad_v), d_bias_out])
    grad_inputs = (
        matmul(grad_q, projection[0].T)
        + matmul(grad_k, projection[1].T)
        + matmul(grad_v, projection[2].T)
    )
    return (d_proj, d_out, d_bias, grad_inputs)


def ffn_forward(inputs_low, w_in, b_in, w_out, b_out):
    hidden = matmul(inputs_low, w_in) + b_in
    activated = smooth(hidden).astype(jnp.bfloat16)
    return (hidden, activated, matmul(activated, w_out) + b_out)


def ffn_back(inputs_low, hidden, activated, w_in, w_out, grad):
    grad_low = grad.astype(jnp.bfloat16)
    grad_active = matmul(grad_low, w_out.T)
    unused, puller = jax.vjp(smooth, hidden)
    grad_hidden = puller(grad_active)[0].astype(jnp.bfloat16)
    weight_grads = (
        matmul(inputs_low.T, grad_hidden),
        bias_sum(grad_hidden),
        matmul(activated.T, grad_low),
        bias_sum(grad_low),
    )
    return (weight_grads, matmul(grad_hidden, w_in.T))


def cross_keys(memory_low, c_proj, c_bias):
    key_rows = matmul(memory_low, c_proj[1]).astype(jnp.bfloat16)
    values = (matmul(memory_low, c_proj[2]) + c_bias[1]).astype(jnp.bfloat16)
    return jnp.stack([key_rows, values])


def cross_keys_back(memory_low, grad_keys, grad_values, c_proj):
    grad_memory = (matmul(grad_keys, c_proj[1].T) + matmul(grad_values, c_proj[2].T)).astype(
        jnp.bfloat16
    )
    return (
        matmul(memory_low.T, grad_keys),
        matmul(memory_low.T, grad_values),
        bias_sum(grad_values),
        grad_memory,
    )


def encoder_forward(embedded, length, layer):
    projection, out_w, bias_rows, w_in, b_in, w_out, b_out, gain_rows, offsets = layer
    inputs = embedded.astype(jnp.float32)
    queries, key_rows, values = self_project(embedded, projection, bias_rows)
    mixed_rows, attn_probs = mix_forward(
        queries, key_rows, values, key_mask(inputs.shape[0], length)
    )
    first_pre = inputs + matmul(mixed_rows, out_w) + bias_rows[2]
    first_out = layer_norm(first_pre, gain_rows[0], offsets[0])
    first_low = first_out.astype(jnp.bfloat16)
    hidden, activated, ffn_value = ffn_forward(first_low, w_in, b_in, w_out, b_out)
    last_pre = first_out + ffn_value + inputs
    result = layer_norm(last_pre, gain_rows[1], offsets[1])
    saved = (
        embedded,
        queries,
        key_rows,
        values,
        attn_probs,
        mixed_rows,
        first_pre,
        first_low,
        hidden,
        activated,
        last_pre,
    )
    return (result, saved)


def encoder_back(saved, layer, grad_result):
    projection, out_w, bias_rows, w_in, b_in, w_out, b_out, gain_rows, offsets = layer
    (
        embedded,
        queries,
        key_rows,
        values,
        attn_probs,
        mixed_rows,
        first_pre,
        first_low,
        hidden,
        activated,
        last_pre,
    ) = saved
    grad_last, d_gain_last, d_offset_last = norm_back(
        last_pre, gain_rows[1], offsets[1], grad_result
    )
    ffn_grads, grad_first_ffn = ffn_back(first_low, hidden, activated, w_in, w_out, grad_last)
    grad_first = grad_last + grad_first_ffn
    grad_pre, d_gain_first, d_offset_first = norm_back(
        first_pre, gain_rows[0], offsets[0], grad_first
    )
    d_proj, d_out, d_bias, grad_inputs = self_back(
        embedded, projection, out_w, queries, key_rows, values, attn_probs, mixed_rows, grad_pre
    )
    grad_embed = grad_last + grad_pre + grad_inputs
    section_grads = (
        d_proj,
        d_out,
        d_bias,
        ffn_grads[0],
        ffn_grads[1],
        ffn_grads[2],
        ffn_grads[3],
        jnp.stack([d_gain_first, d_gain_last]),
        jnp.stack([d_offset_first, d_offset_last]),
    )
    return (grad_embed, section_grads)


def decoder_step(targets, cot_low, src_len, tgt_len, valid, incoming, layer, cross_set):
    projection, out_w, bias_rows, w_in, b_in, w_out, b_out, gain_rows, offsets = layer
    c_proj, c_out, c_bias, c_gain, c_offset = cross_set
    row_count = targets.shape[0]
    inputs_low = targets.astype(jnp.bfloat16)
    queries, key_rows, values = self_project(inputs_low, projection, bias_rows)
    mixed_rows, attn_probs = mix_forward(queries, key_rows, values, causal_mask(row_count, tgt_len))
    first_pre = targets + matmul(mixed_rows, out_w) + bias_rows[2]
    first_out = layer_norm(first_pre, gain_rows[0], offsets[0])
    first_low = first_out.astype(jnp.bfloat16)
    cross_queries = (matmul(first_low, c_proj[0]) + c_bias[0]).astype(jnp.bfloat16)
    cross_pair = cross_keys(incoming, c_proj, c_bias)
    cross_mixed, cross_probs = mix_forward(
        cross_queries, cross_pair[0], cross_pair[1], key_mask(row_count, src_len)
    )
    second_pre = first_out + matmul(cross_mixed, c_out) + c_bias[2]
    second = layer_norm(second_pre, c_gain, c_offset)
    second_low = second.astype(jnp.bfloat16)
    hidden, activated, ffn_value = ffn_forward(second_low, w_in, b_in, w_out, b_out)
    last_pre = second + ffn_value + targets
    result = layer_norm(last_pre, gain_rows[1], offsets[1])
    shown = (result * valid[:, None]).astype(jnp.bfloat16)
    grad_result = cot_low.astype(jnp.float32) * valid[:, None]
    grad_last, d_gain_last, d_offset_last = norm_back(
        last_pre, gain_rows[1], offsets[1], grad_result
    )
    ffn_grads, grad_second_ffn = ffn_back(second_low, hidden, activated, w_in, w_out, grad_last)
    grad_second = grad_last + grad_second_ffn
    grad_cross_pre, d_cross_gain, d_cross_offset = norm_back(
        second_pre, c_gain, c_offset, grad_second
    )
    d_cross_out, d_cross_bias_out, grad_cross_mixed = output_back(
        cross_mixed, c_out, grad_cross_pre
    )
    grad_cq, grad_ck, grad_cv = mix_back(
        cross_queries, cross_pair[0], cross_pair[1], cross_probs, grad_cross_mixed
    )
    grad_first = grad_cross_pre + matmul(grad_cq, c_proj[0].T)
    d_cross_query = matmul(first_low.T, grad_cq)
    d_keys, d_values, d_bias_values, grad_memory = cross_keys_back(
        incoming, grad_ck, grad_cv, c_proj
    )
    d_cross_proj = jnp.stack([d_cross_query, d_keys, d_values])
    d_cross_bias = jnp.stack([bias_sum(grad_cq), d_bias_values, d_cross_bias_out])
    grad_pre, d_gain_first, d_offset_first = norm_back(
        first_pre, gain_rows[0], offsets[0], grad_first
    )
    d_proj, d_out, d_bias, grad_inputs = self_back(
        inputs_low, projection, out_w, queries, key_rows, values, attn_probs, mixed_rows, grad_pre
    )
    grad_embed = grad_last + grad_pre + grad_inputs
    section_grads = (
        d_proj,
        d_out,
        d_bias,
        ffn_grads[0],
        ffn_grads[1],
        ffn_grads[2],
        ffn_grads[3],
        jnp.stack([d_gain_first, d_gain_last]),
        jnp.stack([d_offset_first, d_offset_last]),
    )
    cross_grads = (d_cross_proj, d_cross_out, d_cross_bias, d_cross_gain, d_cross_offset)
    return (shown, grad_embed, section_grads, cross_grads, grad_memory)


def add_tree(first, second):
    return jax.tree.map(jnp.add, first, second)


def pick(array, index):
    return lax.dynamic_index_in_dim(array, index, 0, keepdims=False)


def place(array, value, index):
    return lax.dynamic_update_index_in_dim(array, value, index, 0)


def per_device(
    embeds,
    cotangent,
    pair_ids,
    seq_lengths,
    alive_count,
    self_proj,
    self_out,
    self_bias,
    ffn_in,
    ffn_in_bias,
    ffn_out,
    ffn_out_bias,
    norm_gain,
    norm_bias,
    cross_proj,
    cross_out,
    cross_bias,
    cross_norm_gain,
    cross_norm_bias,
    pair_embed,
):
    layer = (
        self_proj[0],
        self_out[0],
        self_bias[0],
        ffn_in[0],
        ffn_in_bias[0],
        ffn_out[0],
        ffn_out_bias[0],
        norm_gain[0],
        norm_bias[0],
    )
    cross_set = (cross_proj, cross_out, cross_bias, cross_norm_gain, cross_norm_bias)
    section_zero = lax.axis_index("section") == 0
    local_embeds = embeds[0]
    local_cot = cotangent[0]
    seq_count, row_count, width = local_embeds.shape
    positions = jnp.arange(row_count)
    live_slots = jnp.arange(seq_count) < alive_count[0]
    valid_src = ((positions[None, :] < seq_lengths[0][:, None]) & live_slots[:, None]).astype(
        jnp.float32
    )
    valid_tgt = ((positions[None, :] < seq_lengths[1][:, None]) & live_slots[:, None]).astype(
        jnp.float32
    )
    section_blank = jax.tree.map(lambda weight: jnp.zeros(weight.shape, jnp.float32), layer)
    cross_blank = jax.tree.map(lambda weight: jnp.zeros(weight.shape, jnp.float32), cross_set)
    pair_blank = jnp.zeros(pair_embed.shape, jnp.float32)
    sent_blank = jnp.zeros((row_count, width), jnp.bfloat16)
    pair_onehot = (pair_ids[:, None] == jnp.arange(pair_embed.shape[0])[None, :]).astype(
        jnp.float32
    )
    pair_rows = jnp.dot(pair_onehot, pair_embed, precision=lax.Precision.HIGHEST)

    def encode_at(index):
        result, saved = encoder_forward(
            pick(local_embeds, index), pick(seq_lengths[0], index), layer
        )
        memory_low = result.astype(jnp.bfloat16)
        shown = (result * pick(valid_src, index)[:, None]).astype(jnp.bfloat16)
        return (shown, memory_low)

    def back_at(index, incoming):
        result, saved = encoder_forward(
            pick(local_embeds, index), pick(seq_lengths[0], index), layer
        )
        memory_low = result.astype(jnp.bfloat16)
        grad_result = pick(local_cot, index).astype(jnp.float32) * pick(valid_src, index)[
            :, None
        ] + incoming.astype(jnp.float32)
        grad_embed, section_grads = encoder_back(saved, layer, grad_result)
        return (grad_embed, section_grads, cross_blank)

    def decode_at(index, incoming):
        targets = pick(local_embeds, index).astype(jnp.float32) + pick(pair_rows, index)[None, :]
        return decoder_step(
            targets,
            pick(local_cot, index),
            pick(seq_lengths[0], index),
            pick(seq_lengths[1], index),
            pick(valid_tgt, index),
            incoming,
            layer,
            cross_set,
        )

    def encoder_turn(state, turn, returned):
        out_rows, grad_rows, section_acc, cross_acc, pair_acc = state

        def run_forward(rows):
            index = jnp.minimum(turn, seq_count - 1)
            shown, leaving = encode_at(index)
            return (place(rows, shown, index), leaving)

        def skip_forward(rows):
            return (rows, sent_blank)

        out_rows, forward_sent = lax.cond(turn < seq_count, run_forward, skip_forward, out_rows)

        def run_back(held):
            rows, s_acc, c_acc = held
            index = jnp.clip(turn - 2, 0, seq_count - 1)
            grad_embed, section_grads, cross_grads = back_at(index, returned)
            return (
                place(rows, grad_embed, index),
                add_tree(s_acc, section_grads),
                add_tree(c_acc, cross_grads),
            )

        def skip_back(held):
            return held

        grad_rows, section_acc, cross_acc = lax.cond(
            turn >= 2, run_back, skip_back, (grad_rows, section_acc, cross_acc)
        )
        return ((out_rows, grad_rows, section_acc, cross_acc, pair_acc), forward_sent, sent_blank)

    def decoder_turn(state, turn, arrived):

        def run_decode(held):
            rows, g_rows, s_acc, c_acc, p_acc = held
            index = jnp.clip(turn - 1, 0, seq_count - 1)
            shown, grad_embed, section_grads, cross_grads, leaving = decode_at(index, arrived)
            p_acc = p_acc + pick(pair_onehot, index)[:, None] * jnp.sum(grad_embed, axis=0)[None, :]
            return (
                (
                    place(rows, shown, index),
                    place(g_rows, grad_embed, index),
                    add_tree(s_acc, section_grads),
                    add_tree(c_acc, cross_grads),
                    p_acc,
                ),
                leaving,
            )

        def skip_decode(held):
            return (held, sent_blank)

        state, backward_sent = lax.cond(
            (turn >= 1) & (turn <= seq_count), run_decode, skip_decode, state
        )
        return (state, sent_blank, backward_sent)

    def turn_step(carry, turn):
        state, arrived, returned = carry
        state, forward_sent, backward_sent = lax.cond(
            section_zero,
            lambda: encoder_turn(state, turn, returned),
            lambda: decoder_turn(state, turn, arrived),
        )
        arrived = from_behind(forward_sent, "section", 1)
        returned = from_behind(backward_sent, "section", -1)
        return ((state, arrived, returned), None)

    start_state = (
        jnp.zeros((seq_count, row_count, width), jnp.bfloat16),
        jnp.zeros((seq_count, row_count, width), jnp.float32),
        section_blank,
        cross_blank,
        pair_blank,
    )
    final, unused = lax.scan(
        turn_step, (start_state, sent_blank, sent_blank), jnp.arange(seq_count + 2)
    )
    out_rows, grad_rows, section_total, cross_total, pair_grad = final[0]
    (
        d_proj,
        d_out,
        d_bias,
        d_ffn_in,
        d_ffn_in_bias,
        d_ffn_out,
        d_ffn_out_bias,
        d_gain,
        d_norm_bias,
    ) = section_total
    d_cross_proj, d_cross_out, d_cross_bias, d_cross_gain, d_cross_offset = cross_total
    (
        d_proj,
        d_out,
        d_bias,
        d_ffn_in,
        d_ffn_in_bias,
        d_ffn_out,
        d_ffn_out_bias,
        d_gain,
        d_norm_bias,
    ) = lax.psum(
        (
            d_proj,
            d_out,
            d_bias,
            d_ffn_in,
            d_ffn_in_bias,
            d_ffn_out,
            d_ffn_out_bias,
            d_gain,
            d_norm_bias,
        ),
        "dp",
    )
    d_cross_proj, d_cross_out, d_cross_bias, d_cross_gain, d_cross_offset, pair_grad = lax.psum(
        (d_cross_proj, d_cross_out, d_cross_bias, d_cross_gain, d_cross_offset, pair_grad), "dp"
    )
    d_cross_proj, d_cross_out, d_cross_bias, d_cross_gain, d_cross_offset, pair_grad = (
        lax.psum(d_cross_proj.astype(jnp.bfloat16), "section").astype(jnp.float32),
        lax.psum(d_cross_out.astype(jnp.bfloat16), "section").astype(jnp.float32),
        lax.psum(d_cross_bias.astype(jnp.bfloat16), "section").astype(jnp.float32),
        lax.psum(d_cross_gain.astype(jnp.bfloat16), "section").astype(jnp.float32),
        lax.psum(d_cross_offset.astype(jnp.bfloat16), "section").astype(jnp.float32),
        lax.psum(pair_grad.astype(jnp.bfloat16), "section").astype(jnp.float32),
    )
    return (
        out_rows[None],
        grad_rows[None],
        d_proj[None],
        d_out[None],
        d_bias[None],
        d_ffn_in[None],
        d_ffn_in_bias[None],
        d_ffn_out[None],
        d_ffn_out_bias[None],
        d_gain[None],
        d_norm_bias[None],
        d_cross_proj,
        d_cross_out,
        d_cross_bias,
        d_cross_gain,
        d_cross_offset,
        pair_grad,
    )


def solution(mesh):
    in_specs = (
        P("section", "dp", None, None),
        P("section", "dp", None, None),
        P("dp"),
        P(None, "dp"),
        P("dp"),
        P("section", None, None, None),
        P("section", None, None),
        P("section", None, None),
        P("section", None, None),
        P("section", None),
        P("section", None, None),
        P("section", None),
        P("section", None, None),
        P("section", None, None),
        P(),
        P(),
        P(),
        P(),
        P(),
        P(),
    )
    out_specs = (
        P("section", "dp", None, None),
        P("section", "dp", None, None),
        P("section", None, None, None),
        P("section", None, None),
        P("section", None, None),
        P("section", None, None),
        P("section", None),
        P("section", None, None),
        P("section", None),
        P("section", None, None),
        P("section", None, None),
        P(),
        P(),
        P(),
        P(),
        P(),
        P(),
    )
    return jax.shard_map(
        per_device, mesh=mesh, in_specs=in_specs, out_specs=out_specs, check_vma=False
    )
```

profile of v0, /device:TPU:1, one launch (start us, length us, event | category | flops | bytes accessed | tf_op | source)
XLA Modules:
  0.0 1719.5 jit_solution(6508592724636356072)
XLA Ops:
  11.1 4.1 copy.64
  41.5 1246.9 %while.51 = (s32[]{:T(128)}, bf16[2,1024,512]{1,2,0:T(8,128)(2,1)}, f32[2,1024,512]{1,2,0:T(8,128)}, f32[3,512,512]{2,1,0:T(8,128)}, f32[512,512]{1,0:T(8,128)},...) while((s32[]{:T(128)}, bf16[2,1024,512]{1,2,0:T(8,128)(2,1)}, ...), condition=%wide.region_68.69_spmd.clone.clone, body=%wide.region_0.68_spmd.clone.clone.sunk | while | flops 39196868608 | bytes 1261784448 | solution.py:493
  45.3 103.9 %conditional.7 = (bf16[2,1024,512]{1,2,0:T(8,128)(2,1)}, f32[2,1024,512]{1,2,0:T(8,128)}, f32[3,512,512]{2,1,0:T(8,128)}, f32[512,512]{1,0:T(8,128)}, f32[3,512]...) conditional(s32[]{:T(128)} %convert_element_type.624, ...), branch_computations={%region_1.36_spmd, %region_37.67_spmd} | conditional | flops 39196856320 | bytes 1244989696 | solution.py:477
  58.2 81.2 %conditional.1 = (bf16[2,1024,512]{1,2,0:T(8,128)(2,1)}, bf16[1024,512]{1,0:T(8,128)(2,1)}) conditional(s32[]{:T(128)} %convert_element_type.388, bf16[2,1024,512]{1,2,0:T(8,128)(2,1)} %get-tuple-element.703, (s32[]{:T(128)}, bf16[2,1024,512]{1,2,0:T(8,128)(2,1)}, bf16[3,512,512]{2,1,0:T(8,128)(2,1)}, f32[3,512]{1,0:T(4,128)}, s32[2,2]{1,0:T(2,128)}, ...), branch_computations={%region_38.37_spmd, %region_39.0_spmd} | conditional | flops 8800178176 | bytes 127150336 | solution.py:429
  70.8 18.8 %fusion.277 = (f32[8,1024]{1,0:T(8,128)S(1)}, f32[8,1024,1024]{1,2,0:T(8,128)}) fusion(pred[1024]{0:T(1024)(128)(4,1)S(1)} %iota_compare_fusion.3, bf16[1024,8,64]{0,2,1:T(8,128)(2,1)S(1)} %bitcast.544, bf16[1024,8,64]{0,2,1:T(8,128)(2,1)} %bitcast.546), kind=kOutput, calls=%fused_computation.437 | convolution fusion | flops 1107297280 | bytes 35685376 | tf_op jit(solution)/shard_map/while/body/eval_jaxpr/cond/branch_1_fun/cond/branch_1_fun/sub | solution.py:73
  89.6 12.7 fusion.138
  106.1 27.8 %fusion.279 = (f32[1024]{0:T(1024)S(1)}, f32[1024,512]{0,1:T(8,128)}) fusion(bf16[2,1024,512]{1,2,0:T(8,128)(2,1)} %get-tuple-element.659, s32[]{:T(128)S(6)} %select_n.37, f32[512]{0:T(512)S(1)} %bitcast.529, bf16[2048,512]{1,0:T(8,128)(2,1)} %get-tuple-element.669, f32[2048]{0:T(1024)S(1)} %bitcast.525, bf16[512,2048]{1,0:T(8,128)(2,1)} %get-tuple-element.667, ...), kind=kOutput, calls=%fused_computation.439 | convolution fusion | flops 4440718336 | bytes 11573252 | tf_op jit(solution)/shard_map/while/body/eval_jaxpr/cond/branch_1_fun/cond/branch_1_fun/dot_general | solution.py:20
  139.4 8.4 conditional.2
  151.9 21.7 %collective-permute-done = bf16[1024,512]{1,0:T(8,128)(2,1)S(1)} collective-permute-done((bf16[1024,512]{1,0:T(8,128)(2,1)}, bf16[1024,512]{1,0:T(8,128)(2,1)S(1)}, u32[]{:S(2)}, u32[]{:S(2)}) %collective-permute-start) | collective-permute-done | bytes 1048608 | tf_op jit(solution)/shard_map/while/body/eval_jaxpr/ppermute | solution.py:16
  173.5 3.9 collective-permute-done.1
  182.8 103.6 %conditional.7 = (bf16[2,1024,512]{1,2,0:T(8,128)(2,1)}, f32[2,1024,512]{1,2,0:T(8,128)}, f32[3,512,512]{2,1,0:T(8,128)}, f32[512,512]{1,0:T(8,128)}, f32[3,512]...) conditional(s32[]{:T(128)} %convert_element_type.624, ...), branch_computations={%region_1.36_spmd, %region_37.67_spmd} | conditional | flops 39196856320 | bytes 1244989696 | solution.py:477
  195.2 81.2 %conditional.1 = (bf16[2,1024,512]{1,2,0:T(8,128)(2,1)}, bf16[1024,512]{1,0:T(8,128)(2,1)}) conditional(s32[]{:T(128)} %convert_element_type.388, bf16[2,1024,512]{1,2,0:T(8,128)(2,1)} %get-tuple-element.703, (s32[]{:T(128)}, bf16[2,1024,512]{1,2,0:T(8,128)(2,1)}, bf16[3,512,512]{2,1,0:T(8,128)(2,1)}, f32[3,512]{1,0:T(4,128)}, s32[2,2]{1,0:T(2,128)}, ...), branch_computations={%region_38.37_spmd, %region_39.0_spmd} | conditional | flops 8800178176 | bytes 127150336 | solution.py:429
  207.7 18.9 %fusion.277 = (f32[8,1024]{1,0:T(8,128)S(1)}, f32[8,1024,1024]{1,2,0:T(8,128)}) fusion(pred[1024]{0:T(1024)(128)(4,1)S(1)} %iota_compare_fusion.3, bf16[1024,8,64]{0,2,1:T(8,128)(2,1)S(1)} %bitcast.544, bf16[1024,8,64]{0,2,1:T(8,128)(2,1)} %bitcast.546), kind=kOutput, calls=%fused_computation.437 | convolution fusion | flops 1107297280 | bytes 35685376 | tf_op jit(solution)/shard_map/while/body/eval_jaxpr/cond/branch_1_fun/cond/branch_1_fun/sub | solution.py:73
  226.6 12.9 fusion.138
  243.2 27.6 %fusion.279 = (f32[1024]{0:T(1024)S(1)}, f32[1024,512]{0,1:T(8,128)}) fusion(bf16[2,1024,512]{1,2,0:T(8,128)(2,1)} %get-tuple-element.659, s32[]{:T(128)S(6)} %select_n.37, f32[512]{0:T(512)S(1)} %bitcast.529, bf16[2048,512]{1,0:T(8,128)(2,1)} %get-tuple-element.669, f32[2048]{0:T(1024)S(1)} %bitcast.525, bf16[512,2048]{1,0:T(8,128)(2,1)} %get-tuple-element.667, ...), kind=kOutput, calls=%fused_computation.439 | convolution fusion | flops 4440718336 | bytes 11573252 | tf_op jit(solution)/shard_map/while/body/eval_jaxpr/cond/branch_1_fun/cond/branch_1_fun/dot_general | solution.py:20
  276.4 8.5 conditional.2
  286.4 283.9 %collective-permute-start = (bf16[1024,512]{1,0:T(8,128)(2,1)}, bf16[1024,512]{1,0:T(8,128)(2,1)S(1)}, u32[]{:S(2)}, u32[]{:S(2)}) collective-permute-start(bf16[1024,512]{1,0:T(8,128)(2,1)} %get-tuple-element.1693), channel_id=1, source_target_pairs={{0,16},{1,17},{2,18},{3,19},{4,20},{5,21},{6,22},{7,23},{8,24},{9,... | collective-permute-start | bytes 3145736 | tf_op jit(solution)/shard_map/while/body/eval_jaxpr/ppermute | solution.py:16
  571.6 20.5 %collective-permute-done = bf16[1024,512]{1,0:T(8,128)(2,1)S(1)} collective-permute-done((bf16[1024,512]{1,0:T(8,128)(2,1)}, bf16[1024,512]{1,0:T(8,128)(2,1)S(1)}, u32[]{:S(2)}, u32[]{:S(2)}) %collective-permute-start) | collective-permute-done | bytes 1048608 | tf_op jit(solution)/shard_map/while/body/eval_jaxpr/ppermute | solution.py:16
  592.1 3.8 collective-permute-done.1
  600.9 241.3 %conditional.7 = (bf16[2,1024,512]{1,2,0:T(8,128)(2,1)}, f32[2,1024,512]{1,2,0:T(8,128)}, f32[3,512,512]{2,1,0:T(8,128)}, f32[512,512]{1,0:T(8,128)}, f32[3,512]...) conditional(s32[]{:T(128)} %convert_element_type.624, ...), branch_computations={%region_1.36_spmd, %region_37.67_spmd} | conditional | flops 39196856320 | bytes 1244989696 | solution.py:477
  613.6 14.8 conditional.1
  628.4 212.2 %conditional.2 = ((f32[2,1024,512]{1,2,0:T(8,128)}, f32[3,512,512]{2,1,0:T(8,128)}, f32[512,512]{1,0:T(8,128)}, f32[3,512]{1,0:T(4,128)}, f32[512,2048]{1,0:T(8,...) conditional(s32[]{:T(128)} %convert_element_type.389, ...), branch_computations={%region_46.45_spmd, %region_47.66_spmd} | conditional | flops 26126331904 | bytes 695020160 | solution.py:444
  644.0 19.0 %fusion.294 = (f32[8,1024]{1,0:T(8,128)S(1)}, f32[8,1024,1024]{1,2,0:T(8,128)}) fusion(pred[1024]{0:T(1024)(128)(4,1)S(1)} %iota_compare_fusion.4, bf16[1024,8,64]{0,2,1:T(8,128)(2,1)} %bitcast.423, bf16[1024,8,64]{0,2,1:T(8,128)(2,1)} %bitcast.425), kind=kOutput, calls=%fused_computation.452 | convolution fusion | flops 1107297280 | bytes 35685376 | tf_op jit(solution)/shard_map/while/body/eval_jaxpr/cond/branch_1_fun/cond/branch_1_fun/sub | solution.py:73
  663.0 12.5 fusion.218
  679.2 24.1 %multiply_convert_fusion.10 = (bf16[1024,2048]{1,0:T(8,128)(2,1)S(1)}, f32[1024,2048]{1,0:T(8,128)}, f32[1024,2048]{1,0:T(8,128)}) fusion(f32[2048]{0:T(1024)S(1)} %bitcast.526, bf16[512,2048]{1,0:T(8,128)(2,1)S(1)} %copy-done.131, f32[1024,512]{0,1:T(8,128)S(1)} %get-tuple-element.1369, f32[512]{0:T(512)S(1)} %bitcast.504, f32[512]{0:T(512)S(1)} %bitcast.479, ...), kind=kOutput, calls=%fused_computation.310 | convolution fusion | flops 2288517120 | bytes 25186304 | tf_op jit(solution)/shard_map/while/body/eval_jaxpr/cond/branch_1_fun/cond/branch_1_fun/dot_general | solution.py:20
  703.3 4.0 fusion.296
  709.9 10.7 convert_reduce_fusion.8
  720.6 3.3 convolution_add_fusion.4
  736.2 14.8 convert_reduce_fusion.11
  751.1 3.4 convolution_bitcast_fusion.6
  754.5 21.5 %multiply_reduce_fusion.11 = (f32[8,1024]{1,0:T(8,128)S(1)}, f32[8,1024,1024]{1,2,0:T(8,128)}) fusion(f32[8,1024,1024]{1,2,0:T(8,128)} %get-tuple-element.1367, f32[8,1024]{1,0:T(8,128)S(1)} %get-tuple-element.1366, bf16[1024,8,64]{0,2,1:T(8,128)(2,1)S(1)} %bitcast.542, bf16[1024,8,64]{0,2,1:T(8,128)(2,1)S(1)} %bitcast.536), kind=kOutput, calls=%fused_computation.298 | convolution fusion | flops 1098899456 | bytes 69271552 | tf_op jit(solution)/shard_map/while/body/eval_jaxpr/cond/branch_1_fun/cond/branch_1_fun/qhd,khd->hqk/dot_general | solution.py:92
  776.0 27.9 %multiply_convert_fusion.9 = bf16[8,1024,1024]{1,2,0:T(8,128)(2,1)} fusion(f32[8,1024,1024]{1,2,0:T(8,128)} %get-tuple-element.1375, f32[8,1024]{1,0:T(8,128)S(1)} %get-tuple-element.1374, f32[8,1024,1024]{1,2,0:T(8,128)} %get-tuple-element.1367, f32[8,1024]{1,0:T(8,128)S(1)} %get-tuple-element.1366), kind=kLoop, calls=%fused_computation.297 | loop fusion | flops 33554432 | bytes 83951616 | tf_op jit(solution)/shard_map/while/body/eval_jaxpr/cond/branch_1_fun/cond/branch_1_fun/convert_element_type | solution.py:96
  803.9 11.3 multiply_convert_fusion.11
  815.2 10.1 convert_reduce_fusion.12
  830.9 3.3 fusion.231
  842.2 146.7 %collective-permute-start = (bf16[1024,512]{1,0:T(8,128)(2,1)}, bf16[1024,512]{1,0:T(8,128)(2,1)S(1)}, u32[]{:S(2)}, u32[]{:S(2)}) collective-permute-start(bf16[1024,512]{1,0:T(8,128)(2,1)} %get-tuple-element.1693), channel_id=1, source_target_pairs={{0,16},{1,17},{2,18},{3,19},{4,20},{5,21},{6,22},{7,23},{8,24},{9,... | collective-permute-start | bytes 3145736 | tf_op jit(solution)/shard_map/while/body/eval_jaxpr/ppermute | solution.py:16
  990.3 19.3 %collective-permute-done = bf16[1024,512]{1,0:T(8,128)(2,1)S(1)} collective-permute-done((bf16[1024,512]{1,0:T(8,128)(2,1)}, bf16[1024,512]{1,0:T(8,128)(2,1)S(1)}, u32[]{:S(2)}, u32[]{:S(2)}) %collective-permute-start) | collective-permute-done | bytes 1048608 | tf_op jit(solution)/shard_map/while/body/eval_jaxpr/ppermute | solution.py:16
  1009.6 3.8 collective-permute-done.1
  1018.4 241.3 %conditional.7 = (bf16[2,1024,512]{1,2,0:T(8,128)(2,1)}, f32[2,1024,512]{1,2,0:T(8,128)}, f32[3,512,512]{2,1,0:T(8,128)}, f32[512,512]{1,0:T(8,128)}, f32[3,512]...) conditional(s32[]{:T(128)} %convert_element_type.624, ...), branch_computations={%region_1.36_spmd, %region_37.67_spmd} | conditional | flops 39196856320 | bytes 1244989696 | solution.py:477
  1031.1 14.8 conditional.1
  1045.9 212.2 %conditional.2 = ((f32[2,1024,512]{1,2,0:T(8,128)}, f32[3,512,512]{2,1,0:T(8,128)}, f32[512,512]{1,0:T(8,128)}, f32[3,512]{1,0:T(4,128)}, f32[512,2048]{1,0:T(8,...) conditional(s32[]{:T(128)} %convert_element_type.389, ...), branch_computations={%region_46.45_spmd, %region_47.66_spmd} | conditional | flops 26126331904 | bytes 695020160 | solution.py:444
  1055.3 3.1 add_convert_fusion.13
  1061.5 19.0 %fusion.294 = (f32[8,1024]{1,0:T(8,128)S(1)}, f32[8,1024,1024]{1,2,0:T(8,128)}) fusion(pred[1024]{0:T(1024)(128)(4,1)S(1)} %iota_compare_fusion.4, bf16[1024,8,64]{0,2,1:T(8,128)(2,1)} %bitcast.423, bf16[1024,8,64]{0,2,1:T(8,128)(2,1)} %bitcast.425), kind=kOutput, calls=%fused_computation.452 | convolution fusion | flops 1107297280 | bytes 35685376 | tf_op jit(solution)/shard_map/while/body/eval_jaxpr/cond/branch_1_fun/cond/branch_1_fun/sub | solution.py:73
  1080.6 12.5 fusion.218
  1096.7 24.1 %multiply_convert_fusion.10 = (bf16[1024,2048]{1,0:T(8,128)(2,1)S(1)}, f32[1024,2048]{1,0:T(8,128)}, f32[1024,2048]{1,0:T(8,128)}) fusion(f32[2048]{0:T(1024)S(1)} %bitcast.526, bf16[512,2048]{1,0:T(8,128)(2,1)S(1)} %copy-done.131, f32[1024,512]{0,1:T(8,128)S(1)} %get-tuple-element.1369, f32[512]{0:T(512)S(1)} %bitcast.504, f32[512]{0:T(512)S(1)} %bitcast.479, ...), kind=kOutput, calls=%fused_computation.310 | convolution fusion | flops 2288517120 | bytes 25186304 | tf_op jit(solution)/shard_map/while/body/eval_jaxpr/cond/branch_1_fun/cond/branch_1_fun/dot_general | solution.py:20
  1120.8 4.0 fusion.296
  1127.4 10.7 convert_reduce_fusion.8
  1138.1 3.3 convolution_add_fusion.4
  1153.7 14.8 convert_reduce_fusion.11
  1168.6 3.4 convolution_bitcast_fusion.6
  1172.0 21.5 %multiply_reduce_fusion.11 = (f32[8,1024]{1,0:T(8,128)S(1)}, f32[8,1024,1024]{1,2,0:T(8,128)}) fusion(f32[8,1024,1024]{1,2,0:T(8,128)} %get-tuple-element.1367, f32[8,1024]{1,0:T(8,128)S(1)} %get-tuple-element.1366, bf16[1024,8,64]{0,2,1:T(8,128)(2,1)S(1)} %bitcast.542, bf16[1024,8,64]{0,2,1:T(8,128)(2,1)S(1)} %bitcast.536), kind=kOutput, calls=%fused_computation.298 | convolution fusion | flops 1098899456 | bytes 69271552 | tf_op jit(solution)/shard_map/while/body/eval_jaxpr/cond/branch_1_fun/cond/branch_1_fun/qhd,khd->hqk/dot_general | solution.py:92
  1193.5 27.9 %multiply_convert_fusion.9 = bf16[8,1024,1024]{1,2,0:T(8,128)(2,1)} fusion(f32[8,1024,1024]{1,2,0:T(8,128)} %get-tuple-element.1375, f32[8,1024]{1,0:T(8,128)S(1)} %get-tuple-element.1374, f32[8,1024,1024]{1,2,0:T(8,128)} %get-tuple-element.1367, f32[8,1024]{1,0:T(8,128)S(1)} %get-tuple-element.1366), kind=kLoop, calls=%fused_computation.297 | loop fusion | flops 33554432 | bytes 83951616 | tf_op jit(solution)/shard_map/while/body/eval_jaxpr/cond/branch_1_fun/cond/branch_1_fun/convert_element_type | solution.py:96
  1221.4 11.3 multiply_convert_fusion.11
  1232.7 10.1 convert_reduce_fusion.12
  1248.4 3.3 fusion.231
  1262.4 18.4 %collective-permute-done = bf16[1024,512]{1,0:T(8,128)(2,1)S(1)} collective-permute-done((bf16[1024,512]{1,0:T(8,128)(2,1)}, bf16[1024,512]{1,0:T(8,128)(2,1)S(1)}, u32[]{:S(2)}, u32[]{:S(2)}) %collective-permute-start) | collective-permute-done | bytes 1048608 | tf_op jit(solution)/shard_map/while/body/eval_jaxpr/ppermute | solution.py:16
  1280.8 3.8 collective-permute-done.1
  1289.1 106.5 %all-reduce.11 = (f32[1,3,512]{2,0,1:T(1,128)}, f32[1,2048]{1,0:T(1,128)}, f32[1,512]{1,0:T(1,128)}, f32[1,2,512]{2,1,0:T(2,128)}, f32[1,2,512]{2,1,0:T(2,128)},...) all-reduce(f32[1,3,512]{2,0,1:T(1,128)S(1)} %broadcast_in_dim.220, ...), channel_id=1, replica_groups=mesh['section'=2,'dp'=16] {'dp'}, use_global_device_ids=true, to_apply=%region_71.72 | all-reduce | flops 1065472 | bytes 6405120 | tf_op jit(solution)/shard_map/psum | solution.py:519
  1396.4 3.9 copy.66
  1400.3 5.1 all-reduce.2
  1407.8 5.4 copy.67
  1413.2 48.6 %all-reduce.10.cloned.1.call-done = (bf16[3,512,512]{2,1,0:T(8,128)(2,1)}, bf16[512,512]{1,0:T(8,128)(2,1)}) async-done(((bf16[3,512,512]{2,1,0:T(8,128)(2,1)}, bf16[512,512]{1,0:T(8,128)(2,1)}), (bf16[3,512,512]{2,1,0:T(8,128)(2,1)}, bf16[512,512]{1,0:T(8,128)(2,1)})) %all-reduce.10.cloned.1.call-update) | async-done | bytes 2097168 | tf_op jit(solution)/shard_map/psum | solution.py:537
  1466.1 235.6 %all-reduce.8.cloned.1.call-done = (f32[1,3,512,512]{3,2,1,0:T(8,128)}, f32[1,512,512]{2,1,0:T(8,128)}, f32[1,512,2048]{2,1,0:T(8,128)}, f32[1,2048,512]{2,1,0:T(8,128)}) async-done(((f32[1,3,512,512]{3,2,1,0:T(8,128)}, f32[1,512,512]{2,1,0:T(8,128)}, f32[1,512,2048]{2,1,0:T(8,128)}, f32[1,2048,512]{2,1,0:T(8,128)}), (f32[1,3,512,512]{3,2,1,0:T(8,128)}, f32[1,512,512]{2,1,0:T(8,128)}, ...) | async-done | bytes 12582928 | tf_op jit(solution)/shard_map/psum | solution.py:519
  1701.7 4.0 copy.287
  (374 shorter events, 206.1 us)
Async XLA Ops:
  7.2 10.4 copy-start
  7.2 1454.5 %all-reduce.10.cloned.1.call-start = ((), (), s32[]{:S(2)}) async-start(), calls=%async_computation.1 | async-start | bytes 4194304 | tf_op jit(solution)/shard_map/psum | solution.py:537
  11.1 4.1 copy-start.69
  41.5 3.8 copy-start.88
  58.2 81.2 %copy-start.6 = (bf16[2,1024,512]{1,2,0:T(8,128)(2,1)S(1)}, bf16[2,1024,512]{1,2,0:T(8,128)(2,1)}, u32[]{:S(2)}) copy-start(bf16[2,1024,512]{1,2,0:T(8,128)(2,1)} %get-tuple-element.732) | copy-start | bytes 6291460 | tf_op jit(solution)/shard_map/while/body/eval_jaxpr/cond
  89.6 12.8 copy-start.136
  149.2 24.3 %collective-permute-start = (bf16[1024,512]{1,0:T(8,128)(2,1)}, bf16[1024,512]{1,0:T(8,128)(2,1)S(1)}, u32[]{:S(2)}, u32[]{:S(2)}) collective-permute-start(bf16[1024,512]{1,0:T(8,128)(2,1)} %get-tuple-element.1693), channel_id=1, source_target_pairs={{0,16},{1,17},{2,18},{3,19},{4,20},{5,21},{6,22},{7,23},{8,24},{9,... | collective-permute-start | bytes 3145736 | tf_op jit(solution)/shard_map/while/body/eval_jaxpr/ppermute | solution.py:16
  150.5 26.8 %collective-permute-start.1 = (bf16[1024,512]{1,0:T(8,128)(2,1)}, bf16[1024,512]{1,0:T(8,128)(2,1)S(1)}, u32[]{:S(2)}, u32[]{:S(2)}) collective-permute-start(bf16[1024,512]{1,0:T(8,128)(2,1)} %get-tuple-element.1694), channel_id=1, source_target_pairs={{16,0},{17,1},{18,2},{19,3},{20,4},{21,5},{22,6},{23,7},{24,8},{25... | collective-permute-start | bytes 3145736 | tf_op jit(solution)/shard_map/while/body/eval_jaxpr/ppermute | solution.py:16
  178.9 3.9 copy-start.88
  195.2 81.2 %copy-start.6 = (bf16[2,1024,512]{1,2,0:T(8,128)(2,1)S(1)}, bf16[2,1024,512]{1,2,0:T(8,128)(2,1)}, u32[]{:S(2)}) copy-start(bf16[2,1024,512]{1,2,0:T(8,128)(2,1)} %get-tuple-element.732) | copy-start | bytes 6291460 | tf_op jit(solution)/shard_map/while/body/eval_jaxpr/cond
  226.6 12.9 copy-start.136
  286.4 305.7 %collective-permute-start = (bf16[1024,512]{1,0:T(8,128)(2,1)}, bf16[1024,512]{1,0:T(8,128)(2,1)S(1)}, u32[]{:S(2)}, u32[]{:S(2)}) collective-permute-start(bf16[1024,512]{1,0:T(8,128)(2,1)} %get-tuple-element.1693), channel_id=1, source_target_pairs={{0,16},{1,17},{2,18},{3,19},{4,20},{5,21},{6,22},{7,23},{8,24},{9,... | collective-permute-start | bytes 3145736 | tf_op jit(solution)/shard_map/while/body/eval_jaxpr/ppermute | solution.py:16
  570.3 25.6 %collective-permute-start.1 = (bf16[1024,512]{1,0:T(8,128)(2,1)}, bf16[1024,512]{1,0:T(8,128)(2,1)S(1)}, u32[]{:S(2)}, u32[]{:S(2)}) collective-permute-start(bf16[1024,512]{1,0:T(8,128)(2,1)} %get-tuple-element.1694), channel_id=1, source_target_pairs={{16,0},{17,1},{18,2},{19,3},{20,4},{21,5},{22,6},{23,7},{24,8},{25... | collective-permute-start | bytes 3145736 | tf_op jit(solution)/shard_map/while/body/eval_jaxpr/ppermute | solution.py:16
  597.0 3.9 copy-start.88
  613.6 14.9 copy-start.6
  663.0 12.5 copy-start.137
  679.2 24.1 %copy-start.133 = (bf16[2048,512]{1,0:T(8,128)(2,1)S(1)}, bf16[2048,512]{1,0:T(8,128)(2,1)}, u32[]{:S(2)}) copy-start(bf16[2048,512]{1,0:T(8,128)(2,1)} %get-tuple-element.686) | copy-start | bytes 6291460 | tf_op jit(solution)/shard_map/while/body/eval_jaxpr/cond/branch_1_fun/cond
  679.2 24.1 %copy-start.145 = (f32[1,512]{1,0:T(1,128)S(1)}, f32[1,512]{1,0:T(1,128)}, u32[]{:S(2)}) copy-start(f32[1,512]{1,0:T(1,128)} %get-tuple-element.687) | copy-start | bytes 6148 | tf_op jit(solution)/shard_map/while/body/eval_jaxpr/cond/branch_1_fun/cond
  709.5 14.4 copy-start.10
  709.8 10.7 copy-start.80
  709.8 10.7 copy-start.113
  709.8 10.8 copy-start.50
  720.6 3.4 copy-start.82
  720.6 3.3 copy-start.115
  720.6 3.3 copy-start.153
  724.0 3.7 copy-start.54
  734.5 16.5 copy-start.24
  751.1 3.4 copy-start.148
  751.1 3.4 copy-start.151
  815.2 10.2 copy-start.84
  825.4 4.5 copy-start.86
  825.5 4.5 copy-start.41
  830.0 6.1 copy-start.58
  830.9 5.3 copy-start.18
  842.2 167.4 %collective-permute-start = (bf16[1024,512]{1,0:T(8,128)(2,1)}, bf16[1024,512]{1,0:T(8,128)(2,1)S(1)}, u32[]{:S(2)}, u32[]{:S(2)}) collective-permute-start(bf16[1024,512]{1,0:T(8,128)(2,1)} %get-tuple-element.1693), channel_id=1, source_target_pairs={{0,16},{1,17},{2,18},{3,19},{4,20},{5,21},{6,22},{7,23},{8,24},{9,... | collective-permute-start | bytes 3145736 | tf_op jit(solution)/shard_map/while/body/eval_jaxpr/ppermute | solution.py:16
  989.0 24.4 %collective-permute-start.1 = (bf16[1024,512]{1,0:T(8,128)(2,1)}, bf16[1024,512]{1,0:T(8,128)(2,1)S(1)}, u32[]{:S(2)}, u32[]{:S(2)}) collective-permute-start(bf16[1024,512]{1,0:T(8,128)(2,1)} %get-tuple-element.1694), channel_id=1, source_target_pairs={{16,0},{17,1},{18,2},{19,3},{20,4},{21,5},{22,6},{23,7},{24,8},{25... | collective-permute-start | bytes 3145736 | tf_op jit(solution)/shard_map/while/body/eval_jaxpr/ppermute | solution.py:16
  1014.6 3.9 copy-start.88
  1031.1 14.9 copy-start.6
  1080.5 12.5 copy-start.137
  1096.7 24.1 %copy-start.133 = (bf16[2048,512]{1,0:T(8,128)(2,1)S(1)}, bf16[2048,512]{1,0:T(8,128)(2,1)}, u32[]{:S(2)}) copy-start(bf16[2048,512]{1,0:T(8,128)(2,1)} %get-tuple-element.686) | copy-start | bytes 6291460 | tf_op jit(solution)/shard_map/while/body/eval_jaxpr/cond/branch_1_fun/cond
  1096.7 24.1 %copy-start.145 = (f32[1,512]{1,0:T(1,128)S(1)}, f32[1,512]{1,0:T(1,128)}, u32[]{:S(2)}) copy-start(f32[1,512]{1,0:T(1,128)} %get-tuple-element.687) | copy-start | bytes 6148 | tf_op jit(solution)/shard_map/while/body/eval_jaxpr/cond/branch_1_fun/cond
  1127.0 14.4 copy-start.10
  1127.3 10.7 copy-start.80
  1127.3 10.7 copy-start.113
  1127.3 10.8 copy-start.50
  1138.1 3.4 copy-start.82
  1138.1 3.3 copy-start.115
  1138.1 3.3 copy-start.153
  1141.5 3.7 copy-start.54
  1152.0 16.5 copy-start.24
  1168.6 3.4 copy-start.148
  1168.6 3.4 copy-start.151
  1232.7 10.2 copy-start.84
  1242.9 4.5 copy-start.86
  1243.0 4.5 copy-start.41
  1247.5 6.1 copy-start.58
  1248.4 5.3 copy-start.18
  1248.4 3.3 copy-start.27
  1259.7 21.1 %collective-permute-start = (bf16[1024,512]{1,0:T(8,128)(2,1)}, bf16[1024,512]{1,0:T(8,128)(2,1)S(1)}, u32[]{:S(2)}, u32[]{:S(2)}) collective-permute-start(bf16[1024,512]{1,0:T(8,128)(2,1)} %get-tuple-element.1693), channel_id=1, source_target_pairs={{0,16},{1,17},{2,18},{3,19},{4,20},{5,21},{6,22},{7,23},{8,24},{9,... | collective-permute-start | bytes 3145736 | tf_op jit(solution)/shard_map/while/body/eval_jaxpr/ppermute | solution.py:16
  1261.1 23.5 %collective-permute-start.1 = (bf16[1024,512]{1,0:T(8,128)(2,1)}, bf16[1024,512]{1,0:T(8,128)(2,1)S(1)}, u32[]{:S(2)}, u32[]{:S(2)}) collective-permute-start(bf16[1024,512]{1,0:T(8,128)(2,1)} %get-tuple-element.1694), channel_id=1, source_target_pairs={{16,0},{17,1},{18,2},{19,3},{20,4},{21,5},{22,6},{23,7},{24,8},{25... | collective-permute-start | bytes 3145736 | tf_op jit(solution)/shard_map/while/body/eval_jaxpr/ppermute | solution.py:16
  1395.6 306.0 %all-reduce.8.cloned.1.call-start = ((), (), s32[]{:S(2)}) async-start(), calls=%async_computation | async-start | bytes 25165824 | tf_op jit(solution)/shard_map/psum | solution.py:519
  1701.7 4.0 copy-start.87
  1701.7 5.0 copy-start.62
  1706.7 3.7 copy-start.61
  (41 other events, 76.1 us)
Sparse Core Ops, SparseCore 0:
  1395.8 65.9 all-reduce.9
  1467.5 234.0 all-reduce.7
where the time goes:
time: 1730 us; the launch traced here: 1720 us
  matrix products  473 us (27%)
  starting transfers between devices  439 us (25%)
  waiting for transfers between devices  380 us (22%)
  blocking collectives  112 us (6%)
  loops' own time  106 us (6%)
  local copies, waits for them, and re-layouts  102 us (6%)
  other arithmetic  93.5 us (5%)
    ppermute x8, starting transfers between devices, from_behind(): lax.ppermute(value, axis, [(source, source + steps) for source in range(l...  439 us
    psum x1, waiting for transfers between devices, per_device(): lax.psum((d_proj, d_out, d_bias, d_ffn_in, d_ffn_in_bias, d_ffn_out, d_ff...  236 us
    dot_general x46, matrix products, matmul(): return jnp.dot(left, right, preferred_element_type=jnp.float32)  230 us
    psum x1, blocking collectives, per_device(): lax.psum((d_proj, d_out, d_bias, d_ffn_in, d_ffn_in_bias, d_ffn_out, d_ff...  106 us
    ppermute x8, waiting for transfers between devices, from_behind(): lax.ppermute(value, axis, [(source, source + steps) for source in range(l...  95.1 us
    sub x4, matrix products, mix_forward(): attn_probs = jax.nn.softmax(scores, axis=-1)  75.7 us
    convert_element_type x2, other arithmetic, mix_back(): grad_scores = grad_scores.astype(jnp.bfloat16)  55.9 us
    another operation x4, loops' own time, turn_step(): lax.cond(section_zero, lambda: encoder_turn(state, turn, returned), lambd...  52.5 us
  transfers between devices with their start and end apart: 10, of which 10 were waited for; matrix products, arithmetic and copies ran while one was open for 1% of the time, Pallas kernels for 0%

commit v1 on v0

v1 whole, which is shorter than its diff:
```python
import jax
import jax.numpy as jnp
import numpy as np
from jax import lax
from jax.experimental import pallas as pl
from jax.experimental.pallas import tpu as pltpu
from jax.sharding import PartitionSpec as P

BF = jnp.bfloat16
F32 = jnp.float32
HEADS = 8
EPSILON = 1e-05
BLOCKED = -1e30
RB = 256
NN = (((1,), (0,)), ((), ()))
NT = (((1,), (1,)), ((), ()))
TN = (((0,), (0,)), ((), ()))


def dot(left, right, dims=NN):
    return lax.dot_general(left, right, dims, preferred_element_type=F32)


def row_block(index, size=RB):
    return pl.ds(pl.multiple_of(index * size, size), size)


def loop(count, body):
    def step(index, carry):
        body(index)
        return carry

    lax.fori_loop(0, count, step, 0)


def lanes_of(half):
    lane = lax.broadcasted_iota(jnp.int32, (1, 128), 1)
    inside = (lane // 64) == half
    spare = lane - 64 * (1 - half)
    ones = (~inside) & (spare < 32)
    block = (~inside) & (spare >= 32)
    flag = (~inside) & (spare == 32)
    return tuple(m.astype(F32) for m in (inside, ones, block, flag))


def norm_rows(value):
    centre = jnp.mean(value, -1, keepdims=True)
    centred = value - centre
    rstd = lax.rsqrt(jnp.mean(centred * centred, -1, keepdims=True) + EPSILON)
    return centred * rstd, rstd


def norm_rows_back(normed, rstd, gain, grad):
    scaled = grad * gain
    return rstd * (
        scaled
        - jnp.mean(scaled, -1, keepdims=True)
        - normed * jnp.mean(scaled * normed, -1, keepdims=True)
    )


def gelu_both(hidden):
    size = jnp.abs(hidden)
    t = pl.reciprocal(1.0 + (0.3275911 * 0.7071067811865476) * size)
    bell = jnp.exp(-0.5 * hidden * hidden)
    half = t * (
        0.127414796
        + t * (-0.142248368 + t * (0.7107068705 + t * (-0.7265760135 + t * 0.5307027145)))
    )
    half = half * bell
    phi = jnp.where(hidden < 0, half, 1.0 - half)
    return hidden * phi, phi + hidden * (bell * 0.3989422804014327)


def key_fill(count, length, ones, block):
    position = lax.broadcasted_iota(jnp.int32, (count, 128), 0)
    return ones + jnp.where(position < length, 0.0, BLOCKED) * block


def causal_cut(scores, query_axis):
    query = lax.broadcasted_iota(jnp.int32, scores.shape, query_axis)
    key = lax.broadcasted_iota(jnp.int32, scores.shape, 1 - query_axis)
    return jnp.where(key <= query, scores, BLOCKED)


def mix_forward(queries, keys, values_t, length, causal, mixed_t, lse):
    count = queries.shape[0]
    span = keys.shape[0]
    size = 256 if causal else min(512, count)

    def pair(index):
        cols = row_block(index, 128)
        q = queries[:, cols].astype(F32) * 0.125
        k = keys[:, cols].astype(F32)
        vt = values_t[cols, :]
        lane = lax.broadcasted_iota(jnp.int32, (128, 1), 0)
        qa, ka, va = [], [], []
        for half in range(2):
            inside, ones, block, flag = lanes_of(half)
            qa.append((q * inside + flag).astype(BF))
            ka.append((k * inside + key_fill(span, length, ones, block)).astype(BF))
            va.append(jnp.where((lane // 64) == half, vt.astype(F32), 1.0).astype(BF))
        for part in range(count // size):
            here = slice(part * size, (part + 1) * size)
            for half in range(2):
                if causal:
                    pieces = [(0, part * size, False), (part * size, size, True)]
                else:
                    pieces = [(0, span, False)]
                pieces = [piece for piece in pieces if piece[1]]
                scores = []
                for start, length_k, cut in pieces:
                    s = dot(ka[half][start : start + length_k], qa[half][here], NT)
                    scores.append(causal_cut(s, 1) if cut else s)
                top = jnp.max(scores[0], axis=0, keepdims=True)
                for s in scores[1:]:
                    top = jnp.maximum(top, jnp.max(s, axis=0, keepdims=True))
                total = None
                for (start, length_k, _), s in zip(pieces, scores):
                    probs = jnp.exp(s - top).astype(BF)
                    o = dot(va[half][:, start : start + length_k], probs)
                    total = o if total is None else total + o
                other = 64 * (1 - half)
                mass = total[other : other + 1]
                own = total[64 * half : 64 * half + 64] / mass
                mixed_t[pl.ds(pl.multiple_of(index * 128 + 64 * half, 64), 64), here] = own.astype(BF)
                lse[index * 2 + half, :, here] = top + jnp.log(mass)

    loop(4, pair)


def split3(value):
    high = value.astype(BF).astype(F32)
    middle = (value - high).astype(BF).astype(F32)
    low = (value - high - middle).astype(BF).astype(F32)
    return high, middle, low


def place_matrix():
    out = np.zeros((16, 512), np.float32)
    for half in range(2):
        other = 64 * (1 - half)
        for piece in range(3):
            out[half * 4 + piece, half * 128 + other + piece] = 1
            out[8 + half * 4 + piece, 256 + half * 128 + other + piece] = 1
        out[half * 4 + 3, half * 128 + other + 32] = 1
    return out


def mix_back(queries, keys, values, mixed_t, lse, grad_mixed, place, length, causal, d_q, d_k, d_v):
    count = queries.shape[0]
    span = keys.shape[0]
    size = 256 if causal else min(512, count)

    def pair(index):
        cols = row_block(index, 128)
        q = queries[:, cols].astype(F32) * 0.125
        k_low = keys[:, cols]
        k = k_low.astype(F32)
        v = values[:, cols].astype(F32)
        g_low = grad_mixed[:, cols]
        g = g_low.astype(F32)
        q_t = q.astype(BF).T
        g_t = g_low.T
        product = g_t.astype(F32) * mixed_t[cols, :].astype(F32)
        row = lax.broadcasted_iota(jnp.int32, (16, count), 0)
        spread = jnp.where((row == 3) | (row == 7), 1.0, 0.0)
        for half in range(2):
            shift = -lse[index * 2 + half]
            delta = -jnp.sum(product[64 * half : 64 * half + 64], axis=0, keepdims=True)
            for base, value in ((0, shift), (8, delta)):
                for piece, part in enumerate(split3(value)):
                    spread = jnp.where(row == base + 4 * half + piece, part, spread)
        extra = dot(spread.astype(BF), place[...], TN)
        qa, ka, va, ga = [], [], [], []
        for half in range(2):
            inside, ones, block, flag = lanes_of(half)
            qa.append((q * inside + extra[:, half * 128 : half * 128 + 128]).astype(BF))
            ga.append((g * inside + extra[:, 256 + half * 128 : 384 + half * 128]).astype(BF))
            ka.append((k * inside + key_fill(span, length, ones, block)).astype(BF))
            va.append((v * inside + (1.0 - inside)).astype(BF))
        lane = lax.broadcasted_iota(jnp.int32, (size, 128), 1)
        total_k = [None, None]
        total_v = [None, None]

        def grow(total, value):
            if total is None:
                return value
            if total.shape == value.shape:
                return total + value
            known = total.shape[1]
            return jnp.concatenate([total + value[:, :known], value[:, known:]], axis=1)

        for part in range(count // size):
            here = slice(part * size, (part + 1) * size)
            reach = (part + 1) * size if causal else span
            out_q = []
            for half in range(2):
                s = dot(qa[half][here], ka[half][:reach], NT)
                if causal:
                    if part:
                        s = jnp.concatenate([s[:, : part * size], causal_cut(s[:, part * size :], 0)], axis=1)
                    else:
                        s = causal_cut(s, 0)
                probs = jnp.exp(s)
                grads = dot(ga[half][here], va[half][:reach], NT)
                probs_low = probs.astype(BF)
                d_s = (probs * grads).astype(BF)
                total_v[half] = grow(total_v[half], dot(g_t[:, here], probs_low))
                total_k[half] = grow(total_k[half], dot(q_t[:, here], d_s))
                out_q.append(dot(d_s, k_low[:reach]))
            d_q[here, cols] = (jnp.where(lane < 64, out_q[0], out_q[1]) * 0.125).astype(BF)
        for target, total in ((d_k, total_k), (d_v, total_v)):
            joined = jnp.concatenate([total[0][:64], total[1][64:]], axis=0).astype(BF)
            target[:, cols] = joined.T

    loop(4, pair)


def project(x_low, proj, bias, q_ref, k_ref, v_ref, v_t, low_ref=None):
    def body(index):
        r = row_block(index)
        x = x_low(r)
        q_ref[r] = (dot(x, proj[0]) + bias[0:1]).astype(BF)
        k_ref[r] = dot(x, proj[1]).astype(BF)
        v_ref[r] = (dot(x, proj[2]) + bias[1:2]).astype(BF)

    loop(q_ref.shape[0] // RB, body)
    v_t[...] = v_ref[...].T


def valid_rows(index, limit):
    return (lax.broadcasted_iota(jnp.int32, (RB, 1), 0) + index * RB < limit).astype(F32)


def ffn_rows(z_low, w_in, c_in, w_out, c_out, act_ref, slope_ref, r):
    total = None
    for c in range(w_in.shape[1] // 512):
        cols = slice(c * 512, c * 512 + 512)
        act, slope = gelu_both(dot(z_low, w_in[:, cols]) + c_in[:, cols])
        act = act.astype(BF)
        act_ref[r, cols] = act
        slope_ref[r, cols] = slope.astype(BF)
        part = dot(act, w_out[cols])
        total = part if total is None else total + part
    return total + c_out[...]


def enc_forward_kernel(
    length, x, proj, out_w, bias, w_in, c_in, w_out, c_out, gain, offset,
    memory, shown, q_ref, k_ref, v_ref, mixed_t, lse, normed1, rstd1, act, slope, normed2, rstd2, v_t,
):
    project(lambda r: x[r], proj, bias, q_ref, k_ref, v_ref, v_t)
    mix_forward(q_ref, k_ref, v_t, length[0], False, mixed_t, lse)
    rows_after(x, mixed_t, out_w, bias, w_in, c_in, w_out, c_out, gain, offset, length[1], memory, shown, normed1, rstd1, act, slope, normed2, rstd2)


def rows_after(x, mixed_t, out_w, bias, w_in, c_in, w_out, c_out, gain, offset, limit, memory, shown, normed1, rstd1, act, slope, normed2, rstd2):
    def body(index):
        r = row_block(index)
        xf = x[r].astype(F32)
        n1, s1 = norm_rows(xf + dot(mixed_t[:, r], out_w[...], TN) + bias[2:3])
        normed1[r] = n1.astype(BF)
        rstd1[r] = s1
        y = n1 * gain[0:1] + offset[0:1]
        f = ffn_rows(y.astype(BF), w_in, c_in, w_out, c_out, act, slope, r)
        n2, s2 = norm_rows(y + f + xf)
        normed2[r] = n2.astype(BF)
        rstd2[r] = s2
        result = n2 * gain[1:2] + offset[1:2]
        memory[r] = result.astype(BF)
        shown[r] = (result * valid_rows(index, limit)).astype(BF)

    loop(x.shape[0] // RB, body)


def ffn_back(grad_low, act, slope, z_low, w_in, w_out, d_hidden, d_w1, d_w2, small, first_row, on_rows):
    small[first_row : first_row + 5] = jnp.zeros((5, 512), F32)

    def body(index):
        r = row_block(index)
        g = grad_low[r]
        total = None
        for c in range(4):
            cols = slice(c * 512, c * 512 + 512)
            dh = (dot(g, w_out[cols], NT) * slope[r, cols].astype(F32)).astype(BF)
            d_hidden[r, cols] = dh
            small[first_row + c : first_row + c + 1] += jnp.sum(dh.astype(F32), axis=0, keepdims=True)
            part = dot(dh, w_in[:, cols], NT)
            total = part if total is None else total + part
        small[first_row + 4 : first_row + 5] += jnp.sum(g.astype(F32), axis=0, keepdims=True)
        on_rows(r, total)

    loop(grad_low.shape[0] // RB, body)
    z = z_low[...]
    g = grad_low[...]
    for c in range(4):
        cols = slice(c * 512, c * 512 + 512)
        d_w1[cols] = dot(z, d_hidden[:, cols], TN).astype(BF)
        d_w2[cols] = dot(act[:, cols], g, TN).astype(BF)


def self_back(x_low, proj, out_w, q_ref, k_ref, v_ref, mixed_t, lse, place, length, causal, grad_low, grad_mixed, d_q, d_k, d_v, d_proj, d_out, small, rest):
    grad_mixed[...] = dot(grad_low[...], out_w[...], NT).astype(BF)
    d_out[...] = dot(mixed_t[...], grad_low[...]).astype(BF)
    mix_back(q_ref, k_ref, v_ref, mixed_t, lse, grad_mixed, place, length, causal, d_q, d_k, d_v)
    small[0:1] = jnp.sum(d_q[...].astype(F32), axis=0, keepdims=True)
    small[1:2] = jnp.sum(d_v[...].astype(F32), axis=0, keepdims=True)
    small[2:3] = jnp.sum(grad_low[...].astype(F32), axis=0, keepdims=True)
    x = x_low[...]
    d_proj[0:512] = dot(x, d_q[...], TN).astype(BF)
    d_proj[512:1024] = dot(x, d_k[...], TN).astype(BF)
    d_proj[1024:1536] = dot(x, d_v[...], TN).astype(BF)

    def body(index):
        r = row_block(index)
        rest(r, dot(d_q[r], proj[0], NT) + dot(d_k[r], proj[1], NT) + dot(d_v[r], proj[2], NT))

    loop(x_low.shape[0] // RB, body)


def enc_back_kernel(
    length, x, d_memory, cot, proj, out_w, w_in, w_out, gain, offset, place,
    q_ref, k_ref, v_ref, mixed_t, lse, normed1, rstd1, act, slope, normed2, rstd2,
    d_x, d_proj, d_out, d_w1, d_w2, small,
    last, grad_low, z_low, d_hidden, grad_mixed, d_q, d_k, d_v,
):
    small[...] = jnp.zeros(small.shape, F32)

    def top(index):
        r = row_block(index)
        n2 = normed2[r].astype(F32)
        g = cot[r].astype(F32) * valid_rows(index, length[1]) + d_memory[r].astype(F32)
        small[9:10] += jnp.sum(g * n2, axis=0, keepdims=True)
        small[11:12] += jnp.sum(g, axis=0, keepdims=True)
        g = norm_rows_back(n2, rstd2[r], gain[1:2], g)
        last[r] = g
        grad_low[r] = g.astype(BF)
        z_low[r] = (normed1[r].astype(F32) * gain[0:1] + offset[0:1]).astype(BF)

    loop(x.shape[0] // RB, top)

    def middle(r, grad):
        n1 = normed1[r].astype(F32)
        g = last[r] + grad
        small[8:9] += jnp.sum(g * n1, axis=0, keepdims=True)
        small[10:11] += jnp.sum(g, axis=0, keepdims=True)
        g = norm_rows_back(n1, rstd1[r], gain[0:1], g)
        last[r] = last[r] + g
        grad_mixed[r] = g.astype(BF)

    ffn_back(grad_low, act, slope, z_low, w_in, w_out, d_hidden, d_w1, d_w2, small, 3, middle)
    grad_low[...] = grad_mixed[...]

    def rest(r, grad):
        d_x[r] = last[r] + grad

    self_back(x, proj, out_w, q_ref, k_ref, v_ref, mixed_t, lse, place, length[0], False, grad_low, grad_mixed, d_q, d_k, d_v, d_proj, d_out, small, rest)


def dec_self_kernel(
    length, x, pair_row, proj, out_w, bias, gain, offset,
    x_low, q_ref, k_ref, v_ref, mixed_t, lse, normed1, rstd1, v_t,
):
    def low(r):
        value = (x[r].astype(F32) + pair_row[...]).astype(BF)
        x_low[r] = value
        return value

    project(low, proj, bias, q_ref, k_ref, v_ref, v_t)
    mix_forward(q_ref, k_ref, v_t, length[0], True, mixed_t, lse)

    def body(index):
        r = row_block(index)
        n1, s1 = norm_rows(x[r].astype(F32) + pair_row[...] + dot(mixed_t[:, r], out_w[...], TN) + bias[2:3])
        normed1[r] = n1
        rstd1[r] = s1

    loop(x.shape[0] // RB, body)


def dec_mid_kernel(
    length, x, pair_row, normed1, memory, cot, c_proj, c_out, c_bias, c_gain, c_offset,
    w_in, c_in, w_out, c_out_b, gain, offset, place,
    shown, grad_last, grad_first, d_memory, d_cproj, d_cout, d_w1, d_w2, small,
    y_low, z_low, q_ref, k_ref, v_ref, v_t, mixed_t, lse, normed2, rstd2, act, slope, normed3, rstd3, grad_low, d_hidden, grad_mixed, d_q, d_k, d_v,
):
    count = x.shape[0]
    span = memory.shape[0]
    small[...] = jnp.zeros(small.shape, F32)

    def queries(index):
        r = row_block(index)
        y = (normed1[r] * gain[0:1] + offset[0:1]).astype(BF)
        y_low[r] = y
        q_ref[r] = (dot(y, c_proj[0]) + c_bias[0:1]).astype(BF)

    loop(count // RB, queries)

    def keys(index):
        r = row_block(index)
        m = memory[r]
        k_ref[r] = dot(m, c_proj[1]).astype(BF)
        v_ref[r] = (dot(m, c_proj[2]) + c_bias[1:2]).astype(BF)

    loop(span // RB, keys)
    v_t[...] = v_ref[...].T
    mix_forward(q_ref, k_ref, v_t, length[0], False, mixed_t, lse)

    def forward(index):
        r = row_block(index)
        y = normed1[r] * gain[0:1] + offset[0:1]
        n2, s2 = norm_rows(y + dot(mixed_t[:, r], c_out[...], TN) + c_bias[2:3])
        normed2[r] = n2.astype(BF)
        rstd2[r] = s2
        z = n2 * c_gain[...] + c_offset[...]
        zl = z.astype(BF)
        z_low[r] = zl
        f = ffn_rows(zl, w_in, c_in, w_out, c_out_b, act, slope, r)
        n3, s3 = norm_rows(z + f + x[r].astype(F32) + pair_row[...])
        shown[r] = ((n3 * gain[1:2] + offset[1:2]) * valid_rows(index, length[1])).astype(BF)
        g = cot[r].astype(F32) * valid_rows(index, length[1])
        small[9:10] += jnp.sum(g * n3, axis=0, keepdims=True)
        small[11:12] += jnp.sum(g, axis=0, keepdims=True)
        g = norm_rows_back(n3, s3, gain[1:2], g)
        grad_last[r] = g
        grad_low[r] = g.astype(BF)

    loop(count // RB, forward)

    def middle(r, grad):
        n2 = normed2[r].astype(F32)
        g = grad_last[r] + grad
        small[8:9] += jnp.sum(g * n2, axis=0, keepdims=True)
        small[10:11] += jnp.sum(g, axis=0, keepdims=True)
        g = norm_rows_back(n2, rstd2[r], c_gain[...], g)
        grad_first[r] = g
        grad_mixed[r] = g.astype(BF)

    ffn_back(grad_low, act, slope, z_low, w_in, w_out, d_hidden, d_w1, d_w2, small, 3, middle)
    grad_low[...] = grad_mixed[...]
    grad_mixed[...] = dot(grad_low[...], c_out[...], NT).astype(BF)
    d_cout[...] = dot(mixed_t[...], grad_low[...]).astype(BF)
    mix_back(q_ref, k_ref, v_ref, mixed_t, lse, grad_mixed, place, length[0], False, d_q, d_k, d_v)
    small[0:1] = jnp.sum(d_q[...].astype(F32), axis=0, keepdims=True)
    small[1:2] = jnp.sum(d_v[...].astype(F32), axis=0, keepdims=True)
    small[2:3] = jnp.sum(grad_low[...].astype(F32), axis=0, keepdims=True)
    m = memory[...]
    d_cproj[0:512] = dot(y_low[...], d_q[...], TN).astype(BF)
    d_cproj[512:1024] = dot(m, d_k[...], TN).astype(BF)
    d_cproj[1024:1536] = dot(m, d_v[...], TN).astype(BF)

    def first(index):
        r = row_block(index)
        grad_first[r] += dot(d_q[r], c_proj[0], NT)

    loop(count // RB, first)

    def back(index):
        r = row_block(index)
        d_memory[r] = (dot(d_k[r], c_proj[1], NT) + dot(d_v[r], c_proj[2], NT)).astype(BF)

    loop(span // RB, back)


def dec_self_back_kernel(
    length, x_low, grad_last, grad_first, proj, out_w, gain, place, q_ref, k_ref, v_ref, mixed_t, lse, normed1, rstd1,
    d_x, d_proj, d_out, small,
    last, grad_low, grad_mixed, d_q, d_k, d_v,
):
    small[...] = jnp.zeros(small.shape, F32)

    def top(index):
        r = row_block(index)
        n1 = normed1[r]
        g = grad_first[r]
        small[3:4] += jnp.sum(g * n1, axis=0, keepdims=True)
        small[4:5] += jnp.sum(g, axis=0, keepdims=True)
        g = norm_rows_back(n1, rstd1[r], gain[0:1], g)
        last[r] = grad_last[r] + g
        grad_low[r] = g.astype(BF)

    loop(x_low.shape[0] // RB, top)

    def rest(r, grad):
        g = last[r] + grad
        d_x[r] = g
        small[5:6] += jnp.sum(g, axis=0, keepdims=True)

    self_back(x_low, proj, out_w, q_ref, k_ref, v_ref, mixed_t, lse, place, length[0], True, grad_low, grad_mixed, d_q, d_k, d_v, d_proj, d_out, small, rest)


def vm(shape, dtype):
    return pltpu.VMEM(shape, dtype)


def sds(shape, dtype):
    return jax.ShapeDtypeStruct(shape, dtype)


def call(kernel, name, outs, scratch, length, args, flops=0):
    spec = pl.BlockSpec(memory_space=pltpu.VMEM)
    return pl.pallas_call(
        kernel,
        name=name,
        out_shape=[sds(*o) for o in outs],
        in_specs=[pl.BlockSpec(memory_space=pltpu.SMEM)] + [spec] * len(args),
        out_specs=[spec] * len(outs),
        scratch_shapes=[vm(*s) for s in scratch],
        compiler_params=pltpu.CompilerParams(vmem_limit_bytes=62 * 2**20),
        cost_estimate=pl.CostEstimate(flops=flops, bytes_accessed=20 * 2**20, transcendentals=0),
    )(length, *args)


def enc_forward(length, x, layer):
    proj, out_w, bias, w_in, c_in, w_out, c_out, gain, offset = layer
    n, d = x.shape
    f = w_in.shape[1]
    outs = [((n, d), BF), ((n, d), BF), ((n, d), BF), ((n, d), BF), ((n, d), BF), ((d, n), BF), ((8, 1, n), F32),
            ((n, d), BF), ((n, 1), F32), ((n, f), BF), ((n, f), BF), ((n, d), BF), ((n, 1), F32)]
    res = call(enc_forward_kernel, "encoder_forward", outs, [((d, n), BF)], length,
               [x, proj, out_w, bias, w_in, c_in, w_out, c_out, gain, offset], int(15e9))
    return res[0], res[1], tuple(res[2:])


def enc_back(length, x, d_memory, cot, layer, place, saved):
    proj, out_w, bias, w_in, c_in, w_out, c_out, gain, offset = layer
    n, d = x.shape
    f = w_in.shape[1]
    outs = [((n, d), F32), ((3 * d, d), BF), ((d, d), BF), ((f, d), BF), ((f, d), BF), ((16, d), F32)]
    scratch = [((n, d), F32), ((n, d), BF), ((n, d), BF), ((n, f), BF), ((n, d), BF), ((n, d), BF), ((n, d), BF), ((n, d), BF)]
    return call(enc_back_kernel, "encoder_back", outs, scratch, length,
                [x, d_memory, cot, proj, out_w, w_in, w_out, gain, offset, place, *saved], int(35e9))


def dec_self(length, x, pair_row, layer):
    proj, out_w, bias, w_in, c_in, w_out, c_out, gain, offset = layer
    n, d = x.shape
    outs = [((n, d), BF), ((n, d), BF), ((n, d), BF), ((n, d), BF), ((d, n), BF), ((8, 1, n), F32), ((n, d), F32), ((n, 1), F32)]
    return call(dec_self_kernel, "decoder_self", outs, [((d, n), BF)], length,
                [x, pair_row, proj, out_w, bias, gain, offset], int(8e9))


def dec_mid(length, x, pair_row, normed1, memory, cot, layer, cross, place):
    proj, out_w, bias, w_in, c_in, w_out, c_out, gain, offset = layer
    n, d = x.shape
    m = memory.shape[0]
    f = w_in.shape[1]
    outs = [((n, d), BF), ((n, d), F32), ((n, d), F32), ((m, d), BF), ((3 * d, d), BF), ((d, d), BF), ((f, d), BF), ((f, d), BF), ((16, d), F32)]
    scratch = [((n, d), BF), ((n, d), BF), ((n, d), BF), ((m, d), BF), ((m, d), BF), ((d, m), BF), ((d, n), BF), ((8, 1, n), F32),
               ((n, d), BF), ((n, 1), F32), ((n, f), BF), ((n, f), BF), ((8, 128), F32), ((8, 128), F32), ((n, d), BF), ((n, f), BF), ((n, d), BF),
               ((n, d), BF), ((m, d), BF), ((m, d), BF)]
    return call(dec_mid_kernel, "decoder_middle", outs, scratch, length,
                [x, pair_row, normed1, memory, cot, *cross, w_in, c_in, w_out, c_out, gain, offset, place], int(55e9))


def dec_self_back(length, x_low, grad_last, grad_first, layer, place, saved):
    proj, out_w, bias, w_in, c_in, w_out, c_out, gain, offset = layer
    n, d = x_low.shape
    outs = [((n, d), F32), ((3 * d, d), BF), ((d, d), BF), ((8, d), F32)]
    scratch = [((n, d), F32), ((n, d), BF), ((n, d), BF), ((n, d), BF), ((n, d), BF), ((n, d), BF)]
    return call(dec_self_back_kernel, "decoder_self_back", outs, scratch, length,
                [x_low, grad_last, grad_first, proj, out_w, gain, place, *saved], int(20e9))


def nothing(*refs):
    pass


def blank(*shapes):
    spec = pl.BlockSpec(memory_space=pl.ANY)
    return pl.pallas_call(nothing, name="blank", out_shape=[sds(*s) for s in shapes], out_specs=[spec] * len(shapes))()


def per_device(
    embeds, cotangent, pair_ids, seq_lengths, alive_count,
    self_proj, self_out, self_bias, ffn_in, ffn_in_bias, ffn_out, ffn_out_bias, norm_gain, norm_bias,
    cross_proj, cross_out, cross_bias, cross_norm_gain, cross_norm_bias, pair_embed,
):
    layer = (self_proj[0], self_out[0], self_bias[0], ffn_in[0], ffn_in_bias, ffn_out[0], ffn_out_bias, norm_gain[0], norm_bias[0])
    cross = (cross_proj, cross_out, cross_bias, cross_norm_gain[None], cross_norm_bias[None])
    place = jnp.asarray(place_matrix(), BF)
    section_zero = lax.axis_index("section") == 0
    x, cot = embeds[0], cotangent[0]
    count, n, d = x.shape
    f = ffn_in.shape[2]
    live = (jnp.arange(count) < alive_count[0])[None, :]
    valid = jnp.where(live, seq_lengths, 0)
    pairs = pair_embed.shape[0]
    onehot = (pair_ids[:, None] == jnp.arange(pairs)[None, :]).astype(F32)
    pair_rows = jnp.dot(onehot, pair_embed, precision=lax.Precision.HIGHEST)
    src = [jnp.stack([seq_lengths[0, s], valid[0, s]]) for s in range(count)]
    tgt = [jnp.stack([seq_lengths[1, s], valid[1, s]]) for s in range(count)]
    mid = [jnp.stack([seq_lengths[0, s], valid[1, s]]) for s in range(count)]
    nd, nf, n1 = (n, d), (n, f), (n, 1)

    def first(s):
        def enc():
            memory, shown, (q, k, v, mt, lse, na, ra, act, slope, nb, rb) = enc_forward(src[s], x[s], layer)
            (wide,) = blank((nd, F32))
            return memory, shown, q, k, v, mt, lse, ra, na, wide, act, slope, nb, rb

        def dec():
            low, q, k, v, mt, lse, na, ra = dec_self(tgt[s], x[s], pair_rows[s : s + 1], layer)
            memory, shown, act, slope, nb, rb = blank((nd, BF), (nd, BF), (nf, BF), (nf, BF), (nd, BF), (n1, F32))
            return memory, shown, q, k, v, mt, lse, ra, low, na, act, slope, nb, rb

        return lax.cond(section_zero, enc, dec)

    def middle(s, saved, memory):
        def enc():
            return (saved[1], *blank((nd, F32), (nd, F32), (nd, BF), ((3 * d, d), BF), ((d, d), BF), ((f, d), BF), ((f, d), BF), ((16, d), F32)))

        def dec():
            return tuple(dec_mid(mid[s], x[s], pair_rows[s : s + 1], saved[9], memory, cot[s], layer, cross, place))

        return lax.cond(section_zero, enc, dec)

    def last(s, saved, done, d_memory):
        _, _, q, k, v, mt, lse, ra, na, wide, act, slope, nb, rb = saved

        def enc():
            d_x, dp, do, d1, d2, small = enc_back(src[s], x[s], d_memory, cot[s], layer, place, (q, k, v, mt, lse, na, ra, act, slope, nb, rb))
            return d_x, dp, do, d1, d2, small

        def dec():
            d_x, dp, do, small = dec_self_back(tgt[s], na, done[1], done[2], layer, place, (q, k, v, mt, lse, wide, ra))
            m = done[8]
            own = jnp.concatenate([small[0:3], m[3:8], small[3:4], m[9:10], small[4:5], m[11:12], small[5:6], jnp.zeros((3, d), F32)])
            return d_x, dp, do, done[6], done[7], own

        return lax.cond(section_zero, enc, dec)

    ahead = [(0, 1)]
    behind = [(1, 0)]
    saved, memory, done, grads, d_memory = [], [], [], [], []
    for s in range(count):
        saved.append(first(s))
        memory.append(lax.ppermute(saved[s][0], "section", ahead))
    for s in range(count):
        done.append(middle(s, saved[s], memory[s]))
        d_memory.append(lax.ppermute(done[s][3], "section", behind))
    for s in range(count):
        grads.append(last(s, saved[s], done[s], d_memory[s]))
    shown = jnp.stack([done[s][0] for s in range(count)])
    d_x = jnp.stack([grads[s][0] for s in range(count)])

    def total(parts):
        return sum(p.astype(F32) for p in parts)

    own = total([g[5] for g in grads])
    pack = jnp.concatenate([total([g[i] for g in grads]) for i in (1, 2, 3, 4)] + [own]).astype(BF)
    pair_grad = sum(onehot[s][:, None] * grads[s][5][12:13] for s in range(count))
    mid_small = total([m[8] for m in done])
    pack_cross = jnp.concatenate([total([m[4] for m in done]), total([m[5] for m in done]), mid_small, pair_grad]).astype(BF)
    pack = lax.psum(pack, "dp").astype(F32)
    pack_cross = lax.psum(jnp.where(section_zero, 0, pack_cross), ("section", "dp")).astype(F32)
    a, b, c, e = 3 * d, 4 * d, 4 * d + f, 4 * d + 2 * f
    small = pack[e:]
    w1 = pack[b:c].reshape(f // d, d, d).transpose(1, 0, 2).reshape(d, f)
    cs = pack_cross[4 * d :]
    return (
        shown[None], d_x[None],
        pack[:a].reshape(1, 3, d, d), pack[a:b][None], small[None, 0:3], w1[None], small[3:7].reshape(1, f), pack[c:e][None], small[7:8],
        small[None, 8:10], small[None, 10:12],
        pack_cross[:a].reshape(3, d, d), pack_cross[a:b], cs[0:3], cs[8], cs[10], cs[16 : 16 + pairs],
    )


def solution(mesh):
    s, r = "section", P()
    in_specs = (
        P(s, "dp"), P(s, "dp"), P("dp"), P(None, "dp"), P("dp"),
        P(s), P(s), P(s), P(s), P(s), P(s), P(s), P(s), P(s), r, r, r, r, r, r,
    )
    out_specs = (P(s, "dp"), P(s, "dp"), P(s), P(s), P(s), P(s), P(s), P(s), P(s), P(s), P(s), r, r, r, r, r, r)
    return jax.shard_map(per_device, mesh=mesh, in_specs=in_specs, out_specs=out_specs, check_vma=False)
```

time: 1730 us -> 660 us (0.38)
  matrix products: 473 us -> 0.85 us
  starting transfers between devices: 439 us -> 7.32 us
  Pallas kernels: 0 us -> 183 us
  blocking collectives: 112 us -> 0 us
  loops' own time: 106 us -> 14.3 us
  other arithmetic: 93.5 us -> 32.1 us
  local copies, waits for them, and re-layouts: 102 us -> 48.3 us
  waiting for transfers between devices: 380 us -> 349 us
    ppermute x8 -> x4, starting transfers between devices: 439 us -> 7.24 us  [the longest x2 4.52 us: per_device(): memory.append(lax.ppermute(saved[s][0], 'section', ahead))]
    dot_general x59 -> x1, matrix products: 397 us -> 0.85 us  [per_device(): pair_rows = jnp.dot(onehot, pair_embed, precision=lax.Precision.HIGHEST)]
    pallas_call x0 -> x8, Pallas kernels: none -> 183 us  [the longest x4 183 us: call(): pl.pallas_call(kernel, name=name, out_shape=[sds(*o) for o in outs], in_s...]
    psum x2 -> x0, blocking collectives: 112 us -> none  [the longest x1 106 us: per_device(): lax.psum((d_proj, d_out, d_bias, d_ffn_in, d_ffn_in_bias, d_ffn_out, d_ff...]
    another operation x13 -> x6, loops' own time: 106 us -> 14.3 us  [the longest x2 12.9 us: middle(): return lax.cond(section_zero, enc, dec)]
    sub x4 -> x0, matrix products: 75.7 us -> none  [mix_forward(): attn_probs = jax.nn.softmax(scores, axis=-1)]
    convert_element_type x18 -> x2, other arithmetic: 74 us -> 4.66 us  [the longest x1 4.59 us: per_device(): pack = lax.psum(pack, 'dp').astype(F32)]
    psum x2, waiting for transfers between devices: 284 us -> 255 us  [the longest x1 138 us: per_device(): pack = lax.psum(pack, 'dp').astype(F32)]
  transfers between devices with their start and end apart: 10 -> 6, of which waited for: 10 -> 5; matrix products, arithmetic and copies ran while one was open for 1% -> 5% of each run, Pallas kernels for 0% -> 14%
where the time goes in v1:
time: 660 us; the launch traced here: 651 us
  waiting for transfers between devices  349 us (53%)
  Pallas kernels  183 us (28%)
  local copies, waits for them, and re-layouts  48.3 us (7%)
  other arithmetic  32.1 us (5%)
  between operations  15.4 us (2%)
  loops' own time  14.3 us (2%)
  starting transfers between devices  7.32 us (1%)
    pallas_call x4, Pallas kernels, call(): pl.pallas_call(kernel, name=name, out_shape=[sds(*o) for o in outs], in_s...  183 us
    psum x1, waiting for transfers between devices, per_device(): pack = lax.psum(pack, 'dp').astype(F32)  138 us
    psum x1, waiting for transfers between devices, per_device(): lax.psum(jnp.where(section_zero, 0, pack_cross), ('section', 'dp'))  117 us
    ppermute x2, waiting for transfers between devices, per_device(): d_memory.append(lax.ppermute(done[s][3], 'section', behind))  84.1 us
  transfers between devices with their start and end apart: 6, of which 5 were waited for; matrix products, arithmetic and copies ran while one was open for 5% of the time, Pallas kernels for 14%

profile of v1, /device:TPU:1, one launch (start us, length us, event | category | flops | bytes accessed | tf_op | source)
XLA Modules:
  0.0 650.6 jit_solution(6873148538372998813)
XLA Ops:
  7.3 1.4 fusion.14
  9.3 0.7 broadcast_select_fusion
  10.0 0.6 fusion.13
  10.6 0.7 copy.42
  11.3 1.4 pad_add_fusion.1
  12.7 1.4 pad_add_fusion
  14.0 0.8 fusion.6
  14.9 43.0 %conditional.6 = (bf16[1024,512]{1,0:T(8,128)(2,1)}, bf16[1024,512]{1,0:T(8,128)(2,1)}, bf16[1024,512]{1,0:T(8,128)(2,1)}, bf16[1024,512]{1,0:T(8,128)(2,1)}, bf...) conditional(s32[]{:T(128)} %convert_element_type.69, ...), branch_computations={%region_0.1_spmd, %region_1.2_spmd} | conditional | flops 15000000512 | bytes 25239804 | solution.py:608
  14.9 2.3 slice_bitcast_fusion.1.x
  17.3 40.6 %encoder_forward.2 = (bf16[1024,512]{1,0:T(8,128)(2,1)}, bf16[1024,512]{1,0:T(8,128)(2,1)}, bf16[1024,512]{1,0:T(8,128)(2,1)}, bf16[1024,512]{1,0:T(8,128)(2,1)}...) custom-call(s32[2]{0:T(128)S(1)} %get-tuple-element.374.length, ...), custom_call_target="tpu_custom_call" | custom-call | flops 15000000512 | bytes 20971520 | tf_op jit(solution)/shard_map/cond/branch_1_fun/encoder_forward/pallas_call | solution.py:503
  57.9 2.3 collective-permute-start
  60.1 1.4 pad_add_fusion.3
  61.5 1.9 pad_add_fusion.2
  63.4 42.7 %conditional.8 = (bf16[1024,512]{1,0:T(8,128)(2,1)}, bf16[1024,512]{1,0:T(8,128)(2,1)}, bf16[1024,512]{1,0:T(8,128)(2,1)}, bf16[1024,512]{1,0:T(8,128)(2,1)}, bf...) conditional(s32[]{:T(128)} %convert_element_type.69, ...), branch_computations={%region_4.5_spmd, %region_5.6_spmd} | conditional | flops 15000000512 | bytes 25239804 | solution.py:608
  63.7 2.3 slice_bitcast_fusion.5.x
  66.0 40.1 %encoder_forward.3 = (bf16[1024,512]{1,0:T(8,128)(2,1)}, bf16[1024,512]{1,0:T(8,128)(2,1)}, bf16[1024,512]{1,0:T(8,128)(2,1)}, bf16[1024,512]{1,0:T(8,128)(2,1)}...) custom-call(s32[2]{0:T(128)S(1)} %get-tuple-element.455.length, ...), custom_call_target="tpu_custom_call" | custom-call | flops 15000000512 | bytes 20971520 | tf_op jit(solution)/shard_map/cond/branch_1_fun/encoder_forward/pallas_call | solution.py:503
  106.1 2.3 collective-permute-start.1
  108.4 1.4 pad_add_fusion.4
  109.8 1.4 pad_add_fusion.5
  111.8 7.1 %conditional.7 = (f32[1024,512]{1,0:T(8,128)}, f32[1024,512]{1,0:T(8,128)}, bf16[1024,512]{1,0:T(8,128)(2,1)}, bf16[2048,512]{1,0:T(8,128)(2,1)}, bf16[2048,512]...) conditional(s32[]{:T(128)} %convert_element_type.69, ...), branch_computations={%region_2.3_spmd, %region_3.4_spmd} | conditional | flops 54999998464 | bytes 25243832 | solution.py:617
  118.8 1.3 collective-permute-start.2
  120.1 10.3 %collective-permute-done.1 = bf16[1024,512]{1,0:T(8,128)(2,1)} collective-permute-done((bf16[1024,512]{1,0:T(8,128)(2,1)}, bf16[1024,512]{1,0:T(8,128)(2,1)}, u32[]{:S(2)}, u32[]{:S(2)}) %collective-permute-start.1) | collective-permute-done | bytes 1048608 | tf_op jit(solution)/shard_map/ppermute | solution.py:639
  130.4 5.9 conditional.9
  136.3 1.4 collective-permute-start.3
  137.8 1.0 add_convert_fusion.4
  138.7 1.9 add_convert_fusion.2
  140.6 52.5 %collective-permute-done.2 = bf16[1024,512]{1,0:T(8,128)(2,1)} collective-permute-done((bf16[1024,512]{1,0:T(8,128)(2,1)}, bf16[1024,512]{1,0:T(8,128)(2,1)}, u32[]{:S(2)}, u32[]{:S(2)}) %collective-permute-start.2) | collective-permute-done | bytes 1048608 | tf_op jit(solution)/shard_map/ppermute | solution.py:642
  193.1 54.7 %conditional.10 = ((f32[1024,512]{1,0:T(8,128)}, bf16[1536,512]{1,0:T(8,128)(2,1)}, bf16[512,512]{1,0:T(8,128)(2,1)}, bf16[2048,512]{1,0:T(8,128)(2,1)}, bf16[20...) conditional(s32[]{:T(128)} %convert_element_type.69, (s32[2]{0:T(128)S(1)}, bf16[1024,512]{1,0:T(8,128)(2,1)}, ...), branch_computations={%region_8.9_spmd, %region_9.10_spmd} | conditional | flops 35000000512 | bytes 25165832 | solution.py:632
  193.6 3.0 slice_bitcast_fusion.8
  196.6 51.1 %encoder_back.2 = (f32[1024,512]{1,0:T(8,128)}, bf16[1536,512]{1,0:T(8,128)(2,1)}, bf16[512,512]{1,0:T(8,128)(2,1)}, bf16[2048,512]{1,0:T(8,128)(2,1)}, bf16[204...) custom-call(s32[2]{0:T(128)S(1)} %get-tuple-element.536.length, bf16[1024,512]{1,0:T(8,128)(2,1)} %get-tuple-element.756.x, ...), custom_call_target="tpu_custom_call" | custom-call | flops 35000000512 | bytes 20971520 | tf_op jit(solution)/shard_map/cond/branch_1_fun/encoder_back/pallas_call | solution.py:503
  247.9 31.6 %collective-permute-done.3 = bf16[1024,512]{1,0:T(8,128)(2,1)} collective-permute-done((bf16[1024,512]{1,0:T(8,128)(2,1)}, bf16[1024,512]{1,0:T(8,128)(2,1)}, u32[]{:S(2)}, u32[]{:S(2)}) %collective-permute-start.3) | collective-permute-done | bytes 1048608 | tf_op jit(solution)/shard_map/ppermute | solution.py:642
  279.5 54.6 %conditional.11 = ((f32[1024,512]{1,0:T(8,128)}, bf16[1536,512]{1,0:T(8,128)(2,1)}, bf16[512,512]{1,0:T(8,128)(2,1)}, bf16[2048,512]{1,0:T(8,128)(2,1)}, bf16[20...) conditional(s32[]{:T(128)} %convert_element_type.69, (s32[2]{0:T(128)}, bf16[1024,512]{1,0:T(8,128)(2,1)}, ...), branch_computations={%region_10.11_spmd, %region_11.12_spmd} | conditional | flops 35000000512 | bytes 25165832 | solution.py:632
  279.7 3.0 slice_bitcast_fusion.10
  282.8 51.1 %encoder_back.3 = (f32[1024,512]{1,0:T(8,128)}, bf16[1536,512]{1,0:T(8,128)(2,1)}, bf16[512,512]{1,0:T(8,128)(2,1)}, bf16[2048,512]{1,0:T(8,128)(2,1)}, bf16[204...) custom-call(s32[2]{0:T(128)S(1)} %get-tuple-element.580.length, bf16[1024,512]{1,0:T(8,128)(2,1)} %get-tuple-element.758.x, ...), custom_call_target="tpu_custom_call" | custom-call | flops 35000000512 | bytes 20971520 | tf_op jit(solution)/shard_map/cond/branch_1_fun/encoder_back/pallas_call | solution.py:503
  334.2 2.5 maximum_select_fusion
  336.7 1.3 copy-done.10
  338.1 3.2 fusion.2
  341.3 0.9 fusion.3
  342.2 2.0 fusion
  344.2 1.0 copy-done.7
  345.3 2.0 fusion.1
  347.2 0.6 fusion.4
  347.9 1.2 copy-done.12
  349.4 1.5 maximum_bitcast_fusion.1
  350.9 0.8 copy-done.8
  351.8 0.6 copy-done.9
  352.4 2.5 maximum_bitcast_fusion
  354.9 117.0 %all-reduce.5.cloned.1.call-done = bf16[2080,512]{1,0:T(8,128)(2,1)} async-done(((bf16[2080,512]{1,0:T(8,128)(2,1)}), bf16[2080,512]{1,0:T(8,128)(2,1)}) %all-reduce.5.cloned.1.call-update) | async-done | bytes 2129936 | tf_op jit(solution)/shard_map/psum | solution.py:657
  471.8 3.7 slice.222
  475.5 1.1 slice.223
  476.6 0.6 slice.227
  477.2 0.6 slice.224
  478.4 138.0 %all-reduce.3.cloned.1.call-done = bf16[6160,512]{1,0:T(8,128)(2,1)} async-done(((bf16[6160,512]{1,0:T(8,128)(2,1)}), bf16[6160,512]{1,0:T(8,128)(2,1)}) %all-reduce.3.cloned.1.call-update) | async-done | bytes 6307856 | tf_op jit(solution)/shard_map/psum | solution.py:656
  616.4 4.6 convert_element_type.78
  621.0 2.6 slice_bitcast_fusion.12
  623.6 1.0 slice_bitcast_fusion.13
  624.6 0.6 slice_bitcast_fusion.15
  625.2 0.6 copy.40
  626.4 4.7 copy.38
  631.1 6.0 broadcast_in_dim_reshape.3
  637.2 0.7 slice.215
  637.9 0.6 broadcast_in_dim.53
  638.5 3.5 slice.213
  642.0 1.3 slice.219
  (96 shorter events, 2.5 us)
Async XLA Ops:
  7.2 6.9 %copy-start = (f32[16,512]{1,0:T(8,128)S(1)}, f32[16,512]{1,0:T(8,128)}, u32[]{:S(2)}) copy-start(f32[16,512]{1,0:T(8,128)} %param.52) | copy-start | bytes 98308
  7.2 464.6 %all-reduce.5.cloned.1.call-start = ((), (), s32[]{:S(2)}) async-start(), calls=%async_computation.1 | async-start | bytes 4259840 | tf_op jit(solution)/shard_map/psum | solution.py:657
  12.7 2.2 copy-start.52
  14.9 2.4 copy-start.21
  14.9 2.4 copy-start.24
  14.9 2.4 copy-start.31
  14.9 2.3 copy-start.38
  14.9 2.3 copy-start.43
  57.9 53.9 %collective-permute-start = (bf16[1024,512]{1,0:T(8,128)(2,1)}, bf16[1024,512]{1,0:T(8,128)(2,1)}, u32[]{:S(2)}, u32[]{:S(2)}) collective-permute-start(bf16[1024,512]{1,0:T(8,128)(2,1)} %get-tuple-element.678), channel_id=1, source_target_pairs={{0,16},{1,17},{2,18},{3,19},{4,20},{5,21},{6,22},{7,23},{8,24},{9,... | collective-permute-start | bytes 3145736 | tf_op jit(solution)/shard_map/ppermute | solution.py:639
  61.5 1.9 copy-start.54
  63.4 47.8 %copy-start.49 = (s32[2]{0:T(128)S(1)}, s32[2]{0:T(128)}, u32[]{:S(2)}) copy-start(s32[2]{0:T(128)} %param.35) | copy-start | bytes 28
  63.4 48.4 %copy-start.18 = (bf16[512,512]{1,0:T(8,128)(2,1)S(1)}, bf16[512,512]{1,0:T(8,128)(2,1)}, u32[]{:S(2)}) copy-start(bf16[512,512]{1,0:T(8,128)(2,1)} %param.48) | copy-start | bytes 1572868
  63.4 48.4 %copy-start.28 = (f32[3,512]{1,0:T(4,128)S(1)}, f32[3,512]{1,0:T(4,128)}, u32[]{:S(2)}) copy-start(f32[3,512]{1,0:T(4,128)} %param.49) | copy-start | bytes 18436
  63.4 48.4 %copy-start.47 = (f32[512]{0:T(512)S(1)}, f32[512]{0:T(512)}, u32[]{:S(2)}) copy-start(f32[512]{0:T(512)} %param.50) | copy-start | bytes 6148
  63.4 48.4 %copy-start.48 = (f32[512]{0:T(512)S(1)}, f32[512]{0:T(512)}, u32[]{:S(2)}) copy-start(f32[512]{0:T(512)} %param.51) | copy-start | bytes 6148
  63.4 48.4 %copy-start.51 = (bf16[16,512]{1,0:T(8,128)(2,1)S(1)}, bf16[16,512]{1,0:T(8,128)(2,1)}, u32[]{:S(2)}) copy-start(bf16[16,512]{1,0:T(8,128)(2,1)} %constant.16.clone) | copy-start | bytes 49156
  63.6 2.4 copy-start.23
  63.6 2.4 copy-start.25
  63.6 2.4 copy-start.33
  63.6 2.4 copy-start.40
  63.6 2.3 copy-start.44
  106.1 24.3 %collective-permute-start.1 = (bf16[1024,512]{1,0:T(8,128)(2,1)}, bf16[1024,512]{1,0:T(8,128)(2,1)}, u32[]{:S(2)}, u32[]{:S(2)}) collective-permute-start(bf16[1024,512]{1,0:T(8,128)(2,1)} %get-tuple-element.682), channel_id=1, source_target_pairs={{0,16},{1,17},{2,18},{3,19},{4,20},{5,21},{6,22},{7,23},{8,24},{9,... | collective-permute-start | bytes 3145736 | tf_op jit(solution)/shard_map/ppermute | solution.py:639
  118.8 74.3 %collective-permute-start.2 = (bf16[1024,512]{1,0:T(8,128)(2,1)}, bf16[1024,512]{1,0:T(8,128)(2,1)}, u32[]{:S(2)}, u32[]{:S(2)}) collective-permute-start(bf16[1024,512]{1,0:T(8,128)(2,1)} %get-tuple-element.697), channel_id=1, source_target_pairs={{16,0},{17,1},{18,2},{19,3},{20,4},{21,5},{22,6},{23,7},{24,8},{25... | collective-permute-start | bytes 3145736 | tf_op jit(solution)/shard_map/ppermute | solution.py:642
  136.3 2.4 copy-start.11
  136.3 143.2 %collective-permute-start.3 = (bf16[1024,512]{1,0:T(8,128)(2,1)}, bf16[1024,512]{1,0:T(8,128)(2,1)}, u32[]{:S(2)}, u32[]{:S(2)}) collective-permute-start(bf16[1024,512]{1,0:T(8,128)(2,1)} %get-tuple-element.715), channel_id=1, source_target_pairs={{16,0},{17,1},{18,2},{19,3},{20,4},{21,5},{22,6},{23,7},{24,8},{25... | collective-permute-start | bytes 3145736 | tf_op jit(solution)/shard_map/ppermute | solution.py:642
  138.7 54.4 %copy-start.29 = (f32[1,2,512]{2,1,0:T(2,128)S(1)}, f32[1,2,512]{2,1,0:T(2,128)}, u32[]{:S(2)}) copy-start(f32[1,2,512]{2,1,0:T(2,128)} %param.45) | copy-start | bytes 12292
  138.7 54.4 %copy-start.36 = (f32[1,2,512]{2,1,0:T(2,128)S(1)}, f32[1,2,512]{2,1,0:T(2,128)}, u32[]{:S(2)}) copy-start(f32[1,2,512]{2,1,0:T(2,128)} %param.46) | copy-start | bytes 12292
  138.7 54.4 %copy-start.53 = (s32[2]{0:T(128)S(1)}, s32[2]{0:T(128)}, u32[]{:S(2)}) copy-start(s32[2]{0:T(128)} %copy-done.52) | copy-start | bytes 28
  193.1 86.4 %copy-start.50 = (f32[8,1,1024]{2,1,0:T(1,128)S(1)}, f32[8,1,1024]{2,1,0:T(1,128)}, u32[]{:S(2)}) copy-start(f32[8,1,1024]{2,1,0:T(1,128)} %get-tuple-element.710) | copy-start | bytes 98308
  193.1 86.4 %copy-start.55 = (s32[2]{0:T(128)S(1)}, s32[2]{0:T(128)}, u32[]{:S(2)}) copy-start(s32[2]{0:T(128)} %copy-done.54) | copy-start | bytes 28
  279.5 54.6 %copy-start.16 = (f32[16]{0:T(128)S(1)}, f32[16]{0:T(128)}, u32[]{:S(2)}) copy-start(f32[16]{0:T(128)} %get-tuple-element.763) | copy-start | bytes 196
  279.5 54.6 %copy-start.17 = (f32[16]{0:T(128)S(1)}, f32[16]{0:T(128)}, u32[]{:S(2)}) copy-start(f32[16]{0:T(128)} %get-tuple-element.764) | copy-start | bytes 196
  336.7 1.4 copy-start.10
  336.7 4.6 copy-start.15
  336.7 279.7 %all-reduce.3.cloned.1.call-start = ((), (), s32[]{:S(2)}) async-start(), calls=%async_computation | async-start | bytes 12615680 | tf_op jit(solution)/shard_map/psum | solution.py:656
  338.1 3.2 copy-start.14
  338.1 4.1 copy-start.4
  338.1 4.1 copy-start.6
  342.2 2.0 copy-start.5
  342.2 3.0 copy-start.7
  347.8 1.2 copy-start.12
  347.8 1.6 copy-start.13
  349.4 2.4 copy-start.8
  349.4 3.0 copy-start.9
  471.8 3.7 copy-start.3
  621.0 4.8 copy-start.2
  637.9 5.4 copy-start.1
Sparse Core Ops, SparseCore 0:
  336.8 134.9 all-reduce.4
  476.0 140.3 all-reduce.2

commit v2 on v1

--- a/solution.py
+++ b/solution.py
@@ -1,3 +1,5 @@
+import functools
+
 import jax
 import jax.numpy as jnp
 import numpy as np
@@ -9,6 +11,8 @@
 BF = jnp.bfloat16
 F32 = jnp.float32
 HEADS = 8
+PAIRS = 16
+MESH = pl.DeviceIdType.MESH
 EPSILON = 1e-05
 BLOCKED = -1e30
 RB = 256
@@ -274,9 +278,18 @@
     loop(x.shape[0] // RB, body)
 
 
-def ffn_back(grad_low, act, slope, z_low, w_in, w_out, d_hidden, d_w1, d_w2, small, first_row, on_rows):
-    small[first_row : first_row + 5] = jnp.zeros((5, 512), F32)
-
+def put(target, rows, value, later):
+    target[rows] = (value + target[rows].astype(F32) if later else value).astype(BF)
+
+
+def carry_on(later, before, targets, sems):
+    copies = [pltpu.make_async_copy(b, t, sems.at[i]) for i, (b, t) in enumerate(zip(before, targets))] if later else []
+    for copy in copies:
+        copy.start()
+    return copies
+
+
+def ffn_back(grad_low, act, slope, z_low, w_in, w_out, d_hidden, pack, copies, small, first_row, on_rows):
     def body(index):
         r = row_block(index)
         g = grad_low[r]
@@ -294,23 +307,29 @@
     loop(grad_low.shape[0] // RB, body)
     z = z_low[...]
     g = grad_low[...]
+    for copy in copies:
+        copy.wait()
+    prev = bool(copies)
     for c in range(4):
         cols = slice(c * 512, c * 512 + 512)
-        d_w1[cols] = dot(z, d_hidden[:, cols], TN).astype(BF)
-        d_w2[cols] = dot(act[:, cols], g, TN).astype(BF)
-
-
-def self_back(x_low, proj, out_w, q_ref, k_ref, v_ref, mixed_t, lse, place, length, causal, grad_low, grad_mixed, d_q, d_k, d_v, d_proj, d_out, small, rest):
+        put(pack, cols, dot(z, d_hidden[:, cols], TN), prev)
+        put(pack, slice(2048 + c * 512, 2560 + c * 512), dot(act[:, cols], g, TN), prev)
+
+
+def self_back(x_low, proj, out_w, q_ref, k_ref, v_ref, mixed_t, lse, place, length, causal, grad_low, grad_mixed, d_q, d_k, d_v, pack, copies, small, rest):
+    for copy in copies:
+        copy.wait()
+    prev = bool(copies)
     grad_mixed[...] = dot(grad_low[...], out_w[...], NT).astype(BF)
-    d_out[...] = dot(mixed_t[...], grad_low[...]).astype(BF)
+    put(pack, slice(1536, 2048), dot(mixed_t[...], grad_low[...]), prev)
     mix_back(q_ref, k_ref, v_ref, mixed_t, lse, grad_mixed, place, length, causal, d_q, d_k, d_v)
-    small[0:1] = jnp.sum(d_q[...].astype(F32), axis=0, keepdims=True)
-    small[1:2] = jnp.sum(d_v[...].astype(F32), axis=0, keepdims=True)
-    small[2:3] = jnp.sum(grad_low[...].astype(F32), axis=0, keepdims=True)
+    small[0:1] += jnp.sum(d_q[...].astype(F32), axis=0, keepdims=True)
+    small[1:2] += jnp.sum(d_v[...].astype(F32), axis=0, keepdims=True)
+    small[2:3] += jnp.sum(grad_low[...].astype(F32), axis=0, keepdims=True)
     x = x_low[...]
-    d_proj[0:512] = dot(x, d_q[...], TN).astype(BF)
-    d_proj[512:1024] = dot(x, d_k[...], TN).astype(BF)
-    d_proj[1024:1536] = dot(x, d_v[...], TN).astype(BF)
+    put(pack, slice(0, 512), dot(x, d_q[...], TN), prev)
+    put(pack, slice(512, 1024), dot(x, d_k[...], TN), prev)
+    put(pack, slice(1024, 1536), dot(x, d_v[...], TN), prev)
 
     def body(index):
         r = row_block(index)
@@ -320,12 +339,15 @@
 
 
 def enc_back_kernel(
-    length, x, d_memory, cot, proj, out_w, w_in, w_out, gain, offset, place,
-    q_ref, k_ref, v_ref, mixed_t, lse, normed1, rstd1, act, slope, normed2, rstd2,
-    d_x, d_proj, d_out, d_w1, d_w2, small,
-    last, grad_low, z_low, d_hidden, grad_mixed, d_q, d_k, d_v,
+    later, length, x, d_memory, cot, proj, out_w, w_in, w_out, gain, offset, place,
+    q_ref, k_ref, v_ref, mixed_t, lse, normed1, rstd1, act, slope, normed2, rstd2, *refs,
 ):
-    small[...] = jnp.zeros(small.shape, F32)
+    d_x, pack_a, pack_b, small, last, grad_low, z_low, d_hidden, grad_mixed, d_q, d_k, d_v, sems = refs[3 * later :]
+    copies = carry_on(later, refs[:3], (small, pack_b, pack_a), sems)
+    if later:
+        copies[0].wait()
+    else:
+        small[...] = jnp.zeros(small.shape, F32)
 
     def top(index):
         r = row_block(index)
@@ -349,13 +371,13 @@
         last[r] = last[r] + g
         grad_mixed[r] = g.astype(BF)
 
-    ffn_back(grad_low, act, slope, z_low, w_in, w_out, d_hidden, d_w1, d_w2, small, 3, middle)
+    ffn_back(grad_low, act, slope, z_low, w_in, w_out, d_hidden, pack_b, copies[1:2], small, 3, middle)
     grad_low[...] = grad_mixed[...]
 
     def rest(r, grad):
         d_x[r] = last[r] + grad
 
-    self_back(x, proj, out_w, q_ref, k_ref, v_ref, mixed_t, lse, place, length[0], False, grad_low, grad_mixed, d_q, d_k, d_v, d_proj, d_out, small, rest)
+    self_back(x, proj, out_w, q_ref, k_ref, v_ref, mixed_t, lse, place, length[0], False, grad_low, grad_mixed, d_q, d_k, d_v, pack_a, copies[-1:], small, rest)
 
 
 def dec_self_kernel(
@@ -380,14 +402,20 @@
 
 
 def dec_mid_kernel(
-    length, x, pair_row, normed1, memory, cot, c_proj, c_out, c_bias, c_gain, c_offset,
-    w_in, c_in, w_out, c_out_b, gain, offset, place,
-    shown, grad_last, grad_first, d_memory, d_cproj, d_cout, d_w1, d_w2, small,
-    y_low, z_low, q_ref, k_ref, v_ref, v_t, mixed_t, lse, normed2, rstd2, act, slope, normed3, rstd3, grad_low, d_hidden, grad_mixed, d_q, d_k, d_v,
+    later, length, x, pair_row, normed1, memory, cot, c_proj, c_out, c_bias, c_gain, c_offset,
+    w_in, c_in, w_out, c_out_b, gain, offset, place, *refs,
 ):
+    shown, grad_last, grad_first, d_memory, pack_b, pack_c, small = refs[3 * later : 3 * later + 7]
+    (
+        y_low, z_low, q_ref, k_ref, v_ref, v_t, mixed_t, lse, normed2, rstd2, act, slope, grad_low, d_hidden, grad_mixed, d_q, d_k, d_v, sems,
+    ) = refs[3 * later + 7 :]
+    copies = carry_on(later, refs[:3], (small, pack_b, pack_c), sems)
     count = x.shape[0]
     span = memory.shape[0]
-    small[...] = jnp.zeros(small.shape, F32)
+    if later:
+        copies[0].wait()
+    else:
+        small[...] = jnp.zeros(small.shape, F32)
 
     def queries(index):
         r = row_block(index)
@@ -437,18 +465,20 @@
         grad_first[r] = g
         grad_mixed[r] = g.astype(BF)
 
-    ffn_back(grad_low, act, slope, z_low, w_in, w_out, d_hidden, d_w1, d_w2, small, 3, middle)
+    ffn_back(grad_low, act, slope, z_low, w_in, w_out, d_hidden, pack_b, copies[1:2], small, 3, middle)
     grad_low[...] = grad_mixed[...]
     grad_mixed[...] = dot(grad_low[...], c_out[...], NT).astype(BF)
-    d_cout[...] = dot(mixed_t[...], grad_low[...]).astype(BF)
+    for copy in copies[2:]:
+        copy.wait()
+    put(pack_c, slice(1536, 2048), dot(mixed_t[...], grad_low[...]), later)
     mix_back(q_ref, k_ref, v_ref, mixed_t, lse, grad_mixed, place, length[0], False, d_q, d_k, d_v)
-    small[0:1] = jnp.sum(d_q[...].astype(F32), axis=0, keepdims=True)
-    small[1:2] = jnp.sum(d_v[...].astype(F32), axis=0, keepdims=True)
-    small[2:3] = jnp.sum(grad_low[...].astype(F32), axis=0, keepdims=True)
+    small[0:1] += jnp.sum(d_q[...].astype(F32), axis=0, keepdims=True)
+    small[1:2] += jnp.sum(d_v[...].astype(F32), axis=0, keepdims=True)
+    small[2:3] += jnp.sum(grad_low[...].astype(F32), axis=0, keepdims=True)
     m = memory[...]
-    d_cproj[0:512] = dot(y_low[...], d_q[...], TN).astype(BF)
-    d_cproj[512:1024] = dot(m, d_k[...], TN).astype(BF)
-    d_cproj[1024:1536] = dot(m, d_v[...], TN).astype(BF)
+    put(pack_c, slice(0, 512), dot(y_low[...], d_q[...], TN), later)
+    put(pack_c, slice(512, 1024), dot(m, d_k[...], TN), later)
+    put(pack_c, slice(1024, 1536), dot(m, d_v[...], TN), later)
 
     def first(index):
         r = row_block(index)
@@ -464,18 +494,25 @@
 
 
 def dec_self_back_kernel(
-    length, x_low, grad_last, grad_first, proj, out_w, gain, place, q_ref, k_ref, v_ref, mixed_t, lse, normed1, rstd1,
-    d_x, d_proj, d_out, small,
-    last, grad_low, grad_mixed, d_q, d_k, d_v,
+    later, length, x_low, grad_last, grad_first, proj, out_w, gain, place, q_ref, k_ref, v_ref, mixed_t, lse, normed1, rstd1,
+    middle_small, pair_mark, *refs,
 ):
-    small[...] = jnp.zeros(small.shape, F32)
+    d_x, pack_a, small, last, grad_low, grad_mixed, d_q, d_k, d_v, column, sems = refs[2 * later :]
+    copies = carry_on(later, refs[:2], (small, pack_a), sems)
+    if later:
+        copies[0].wait()
+    else:
+        small[...] = jnp.zeros(small.shape, F32)
+    for here in (3, 4, 5, 6, 7, 9, 11):
+        small[here : here + 1] = middle_small[here : here + 1]
+    column[...] = jnp.zeros(column.shape, F32)
 
     def top(index):
         r = row_block(index)
         n1 = normed1[r]
         g = grad_first[r]
-        small[3:4] += jnp.sum(g * n1, axis=0, keepdims=True)
-        small[4:5] += jnp.sum(g, axis=0, keepdims=True)
+        small[8:9] += jnp.sum(g * n1, axis=0, keepdims=True)
+        small[10:11] += jnp.sum(g, axis=0, keepdims=True)
         g = norm_rows_back(n1, rstd1[r], gain[0:1], g)
         last[r] = grad_last[r] + g
         grad_low[r] = g.astype(BF)
@@ -485,9 +522,10 @@
     def rest(r, grad):
         g = last[r] + grad
         d_x[r] = g
-        small[5:6] += jnp.sum(g, axis=0, keepdims=True)
-
-    self_back(x_low, proj, out_w, q_ref, k_ref, v_ref, mixed_t, lse, place, length[0], True, grad_low, grad_mixed, d_q, d_k, d_v, d_proj, d_out, small, rest)
+        column[0:1] += jnp.sum(g, axis=0, keepdims=True)
+
+    self_back(x_low, proj, out_w, q_ref, k_ref, v_ref, mixed_t, lse, place, length[0], True, grad_low, grad_mixed, d_q, d_k, d_v, pack_a, copies[-1:], small, rest)
+    small[16:] += pair_mark[...] * column[0:1]
 
 
 def vm(shape, dtype):
@@ -498,18 +536,19 @@
     return jax.ShapeDtypeStruct(shape, dtype)
 
 
-def call(kernel, name, outs, scratch, length, args, flops=0):
+def call(kernel, name, outs, scratch, length, args, flops=0, before=()):
     spec = pl.BlockSpec(memory_space=pltpu.VMEM)
+    anywhere = pl.BlockSpec(memory_space=pl.ANY)
     return pl.pallas_call(
         kernel,
         name=name,
         out_shape=[sds(*o) for o in outs],
-        in_specs=[pl.BlockSpec(memory_space=pltpu.SMEM)] + [spec] * len(args),
+        in_specs=[pl.BlockSpec(memory_space=pltpu.SMEM)] + [spec] * len(args) + [anywhere] * len(before),
         out_specs=[spec] * len(outs),
-        scratch_shapes=[vm(*s) for s in scratch],
+        scratch_shapes=[vm(*s) if isinstance(s, tuple) else s for s in scratch],
         compiler_params=pltpu.CompilerParams(vmem_limit_bytes=62 * 2**20),
         cost_estimate=pl.CostEstimate(flops=flops, bytes_accessed=20 * 2**20, transcendentals=0),
-    )(length, *args)
+    )(length, *args, *before)
 
 
 def enc_forward(length, x, layer):
@@ -523,14 +562,14 @@
     return res[0], res[1], tuple(res[2:])
 
 
-def enc_back(length, x, d_memory, cot, layer, place, saved):
+def enc_back(length, x, d_memory, cot, layer, place, saved, prev):
     proj, out_w, bias, w_in, c_in, w_out, c_out, gain, offset = layer
     n, d = x.shape
     f = w_in.shape[1]
-    outs = [((n, d), F32), ((3 * d, d), BF), ((d, d), BF), ((f, d), BF), ((f, d), BF), ((16, d), F32)]
-    scratch = [((n, d), F32), ((n, d), BF), ((n, d), BF), ((n, f), BF), ((n, d), BF), ((n, d), BF), ((n, d), BF), ((n, d), BF)]
-    return call(enc_back_kernel, "encoder_back", outs, scratch, length,
-                [x, d_memory, cot, proj, out_w, w_in, w_out, gain, offset, place, *saved], int(35e9))
+    outs = [((n, d), F32), ((4 * d, d), BF), ((2 * f, d), BF), ((16 + PAIRS, d), F32)]
+    scratch = [((n, d), F32), ((n, d), BF), ((n, d), BF), ((n, f), BF), ((n, d), BF), ((n, d), BF), ((n, d), BF), ((n, d), BF), pltpu.SemaphoreType.DMA((3,))]
+    return call(functools.partial(enc_back_kernel, bool(prev)), "encoder_back", outs, scratch, length,
+                [x, d_memory, cot, proj, out_w, w_in, w_out, gain, offset, place, *saved], int(35e9), prev)
 
 
 def dec_self(length, x, pair_row, layer):
@@ -541,26 +580,259 @@
                 [x, pair_row, proj, out_w, bias, gain, offset], int(8e9))
 
 
-def dec_mid(length, x, pair_row, normed1, memory, cot, layer, cross, place):
+def dec_mid(length, x, pair_row, normed1, memory, cot, layer, cross, place, prev):
     proj, out_w, bias, w_in, c_in, w_out, c_out, gain, offset = layer
     n, d = x.shape
     m = memory.shape[0]
     f = w_in.shape[1]
-    outs = [((n, d), BF), ((n, d), F32), ((n, d), F32), ((m, d), BF), ((3 * d, d), BF), ((d, d), BF), ((f, d), BF), ((f, d), BF), ((16, d), F32)]
+    outs = [((n, d), BF), ((n, d), F32), ((n, d), F32), ((m, d), BF), ((2 * f, d), BF), ((4 * d, d), BF), ((16, d), F32)]
     scratch = [((n, d), BF), ((n, d), BF), ((n, d), BF), ((m, d), BF), ((m, d), BF), ((d, m), BF), ((d, n), BF), ((8, 1, n), F32),
-               ((n, d), BF), ((n, 1), F32), ((n, f), BF), ((n, f), BF), ((8, 128), F32), ((8, 128), F32), ((n, d), BF), ((n, f), BF), ((n, d), BF),
-               ((n, d), BF), ((m, d), BF), ((m, d), BF)]
-    return call(dec_mid_kernel, "decoder_middle", outs, scratch, length,
-                [x, pair_row, normed1, memory, cot, *cross, w_in, c_in, w_out, c_out, gain, offset, place], int(55e9))
-
-
-def dec_self_back(length, x_low, grad_last, grad_first, layer, place, saved):
+               ((n, d), BF), ((n, 1), F32), ((n, f), BF), ((n, f), BF), ((n, d), BF), ((n, f), BF), ((n, d), BF),
+               ((n, d), BF), ((m, d), BF), ((m, d), BF), pltpu.SemaphoreType.DMA((3,))]
+    return call(functools.partial(dec_mid_kernel, bool(prev)), "decoder_middle", outs, scratch, length,
+                [x, pair_row, normed1, memory, cot, *cross, w_in, c_in, w_out, c_out, gain, offset, place], int(55e9), prev)
+
+
+def dec_self_back(length, x_low, grad_last, grad_first, layer, place, saved, middle_small, pair_mark, prev):
     proj, out_w, bias, w_in, c_in, w_out, c_out, gain, offset = layer
     n, d = x_low.shape
-    outs = [((n, d), F32), ((3 * d, d), BF), ((d, d), BF), ((8, d), F32)]
-    scratch = [((n, d), F32), ((n, d), BF), ((n, d), BF), ((n, d), BF), ((n, d), BF), ((n, d), BF)]
-    return call(dec_self_back_kernel, "decoder_self_back", outs, scratch, length,
-                [x_low, grad_last, grad_first, proj, out_w, gain, place, *saved], int(20e9))
+    outs = [((n, d), F32), ((4 * d, d), BF), ((16 + pair_mark.shape[0], d), F32)]
+    scratch = [((n, d), F32), ((n, d), BF), ((n, d), BF), ((n, d), BF), ((n, d), BF), ((n, d), BF), ((8, d), F32), pltpu.SemaphoreType.DMA((2,))]
+    return call(functools.partial(dec_self_back_kernel, bool(prev)), "decoder_self_back", outs, scratch, length,
+                [x_low, grad_last, grad_first, proj, out_w, gain, place, *saved, middle_small, pair_mark], int(20e9), prev)
+
+
+def add_rows(target, start, size, sources):
+    block = max(b for b in range(16, min(size, 96) + 1, 16) if size % b == 0)
+
+    def body(index):
+        here = pl.ds(pl.multiple_of(start + index * block, 16), block)
+        value = 0.0
+        for ref, begin in sources:
+            value = value + ref[pl.ds(pl.multiple_of(begin + index * block, 16), block)].astype(F32)
+        target[here] = value.astype(BF)
+
+    loop(size // block, body)
+
+
+def grad_sum_kernel(count, rows1, rows2, a, b, c, own, mids, out, work, final, inbox, pairbox, load_sem, send_sem, recv_sem):
+    m = count // 2
+    me = lax.axis_index("dp")
+    section = lax.axis_index("section")
+    core = me % 2
+    chip = me // 2
+    decoder = section == 1
+    na, nb, nc = a.shape[0], b.shape[0], c.shape[0]
+    ns, nm = own.shape[0], mids.shape[0]
+    loads = [
+        pltpu.make_async_copy(a, work.at[pl.ds(0, na)], load_sem.at[0]),
+        pltpu.make_async_copy(b, work.at[pl.ds(na, nb)], load_sem.at[1]),
+        pltpu.make_async_copy(c, work.at[pl.ds(rows1, nc)], load_sem.at[2]),
+    ]
+    for copy in loads:
+        copy.start()
+
+    def device_at(place, core):
+        place = place % m
+        turn = place * (1 - core) + ((m - place) % m) * core
+        odd = turn // (m // 2)
+        return 2 * (2 * (turn * (1 - odd) + (m - 1 - turn) * odd) + odd) + core
+
+    turn = (chip // 2) * (1 - chip % 2) + (m - 1 - chip // 2) * (chip % 2)
+    back = (m - turn) % m
+    place = turn * (1 - core) + back * core
+    place_other = turn * core + back * (1 - core)
+    other = me + 1 - 2 * core
+    after = device_at(place + 1, core)
+    before = device_at(place + m - 1, core)
+    barrier = pltpu.get_barrier_semaphore()
+    for device in (after, before, other):
+        pl.semaphore_signal(barrier, inc=1, device_id={"dp": device}, device_id_type=MESH)
+    pl.semaphore_signal(barrier, inc=1, device_id={"section": 1 - section}, device_id_type=MESH)
+    pad1 = rows1 - na - nb
+    work[na + nb : rows1] = jnp.concatenate([own[0:16], jnp.zeros((pad1 - 16, own.shape[1]), F32)]).astype(BF)
+    pad2 = rows2 - nc
+    work[rows1 + nc : rows1 + rows2] = jnp.concatenate(
+        [mids[...], own[16:], jnp.zeros((pad2 - nm - ns + 16, own.shape[1]), F32)]
+    ).astype(BF)
+    for copy in loads:
+        copy.wait()
+    pl.semaphore_wait(barrier, 4)
+
+    starts, chunks = (0, rows1), (rows1 // count, rows2 // count)
+    units = []
+    for region in range(2):
+        first = chunks[region] // 32 * 16
+        units += [(region, 0, first), (region, first, chunks[region] - first)]
+    boxes, width = [], 0
+    for _, _, size in units:
+        boxes.append(width)
+        width += size
+
+    def low(region, half, chunk):
+        return starts[region] + half * (m * chunks[region]) + (chunk % m) * chunks[region]
+
+    slot = iter(range(10**6))
+
+    def remote(src, dst, device):
+        index = next(slot)
+        return pltpu.make_async_remote_copy(
+            src, dst, send_sem.at[index], recv_sem.at[index], device_id=device, device_id_type=MESH
+        )
+
+    def rows(ref, start, size):
+        return ref.at[pl.ds(pl.multiple_of(start, 16), size)]
+
+    def on_decoder(region, action):
+        if region == 0:
+            action()
+        else:
+            pl.when(decoder)(action)
+
+    def pair_copy(region, t):
+        size = chunks[region]
+        start = low(region, 1 - core, place_other + 2 * m - 1 - t)
+        return remote(rows(work, start, size), rows(pairbox, start - (1 - core) * m * size - starts[region] + (region * m * chunks[0]), size), {"dp": other})
+
+    def pair_low(region, chunk):
+        return region * m * chunks[0] + (chunk % m) * chunks[region]
+
+    pairs = [[pair_copy(region, t) for region in range(2)] for t in range(m)]
+    for t in range(m):
+        for region in range(2):
+            on_decoder(region, pairs[t][region].start)
+    sends = [[None] * len(units) for _ in range(m - 1)]
+    for s in range(m - 1):
+        for u, (region, offset, size) in enumerate(units):
+            start = low(region, core, place + 2 * m - 1 - s) + offset
+            sends[s][u] = remote(rows(work, start, size), inbox.at[pl.ds(s * width + boxes[u], size)], {"dp": after})
+    for t in range(m):
+        for region in range(2):
+            on_decoder(region, pairs[t][region].wait_recv)
+        for u, (region, offset, size) in enumerate(units):
+            chunk = place + 2 * m - 1 - t
+
+            def step(t=t, u=u, region=region, offset=offset, size=size, chunk=chunk):
+                start = low(region, core, chunk) + offset
+                sources = [(work, start), (pairbox, pair_low(region, chunk) + offset)]
+                if t:
+                    sends[t - 1][u].wait_recv()
+                    sources.append((inbox, (t - 1) * width + boxes[u]))
+                add_rows(work if t < m - 1 else final, start, size, sources)
+                if t < m - 1:
+                    sends[t][u].start()
+
+            on_decoder(region, step)
+
+    mine = rows(final, low(1, core, place), chunks[1])
+    across = remote(mine, mine, {"section": 1 - section})
+    pl.when(decoder)(across.start)
+    passes = [[None] * len(units) for _ in range(m - 1)]
+    for s in range(m - 1):
+        for u, (region, offset, size) in enumerate(units):
+            here = rows(final, low(region, core, place + 2 * m - s) + offset, size)
+            passes[s][u] = remote(here, here, {"dp": after})
+    shares = []
+    for s in range(m):
+        for region in range(2):
+            here = rows(final, low(region, core, place + 2 * m - s), chunks[region])
+            shares.append(remote(here, here, {"dp": other}))
+    for s in range(m):
+        for u, (region, offset, size) in enumerate(units):
+            if s:
+                passes[s - 1][u].wait_recv()
+            elif u == 2:
+                pl.when(section == 0)(across.wait_recv)
+            if s < m - 1:
+                passes[s][u].start()
+            if offset:
+                shares[2 * s + region].start()
+    for copy in shares:
+        copy.wait_recv()
+    copy = pltpu.make_async_copy(final, out, load_sem.at[0])
+    copy.start()
+    for t in range(m):
+        for region in range(2):
+            on_decoder(region, pairs[t][region].wait_send)
+    for s in range(m - 1):
+        for u, (region, _, _) in enumerate(units):
+            on_decoder(region, sends[s][u].wait_send)
+            passes[s][u].wait_send()
+    for share in shares:
+        share.wait_send()
+    pl.when(decoder)(across.wait_send)
+    copy.wait()
+
+
+def grad_sum(count, a, b, c, own, mids):
+    d = a.shape[1]
+    unit = 16 * count
+    m = count // 2
+    rows1 = -(-(a.shape[0] + b.shape[0] + 16) // unit) * unit
+    rows2 = -(-(c.shape[0] + own.shape[0] - 16 + mids.shape[0]) // unit) * unit
+    width = (rows1 + rows2) // count
+    slots = (m - 1) * 8 + m * 4 + 1
+    anywhere = pl.BlockSpec(memory_space=pl.ANY)
+    inside = pl.BlockSpec(memory_space=pltpu.VMEM)
+    out = pl.pallas_call(
+        functools.partial(grad_sum_kernel, count, rows1, rows2),
+        name="gradient_sum",
+        out_shape=sds((rows1 + rows2, d), BF),
+        in_specs=[anywhere] * 3 + [inside] * 2,
+        out_specs=anywhere,
+        scratch_shapes=[
+            vm((rows1 + rows2, d), BF),
+            vm((rows1 + rows2, d), BF),
+            vm(((m - 1) * width, d), BF),
+            vm((m * width, d), BF),
+            pltpu.SemaphoreType.DMA((3,)),
+            pltpu.SemaphoreType.DMA((slots,)),
+            pltpu.SemaphoreType.DMA((slots,)),
+        ],
+        compiler_params=pltpu.CompilerParams(collective_id=0, has_side_effects=True, vmem_limit_bytes=48 * 2**20),
+    )(a, b, c, own, mids)
+    return out, rows1
+
+
+def unpack_kernel(rows1, f, pack, proj, out_w, bias, w_in, b_in, w_out, b_out, gain, offset, c_proj, c_out, c_bias, c_gain, c_offset, pair):
+    d = pack.shape[1]
+
+    def put_rows(target, start, size):
+        target[...] = pack[start : start + size].astype(F32)
+
+    put_rows(proj, 0, 3 * d)
+    put_rows(out_w, 3 * d, d)
+    for c in range(f // d):
+        w_in[:, c * d : (c + 1) * d] = pack[(4 + c) * d : (5 + c) * d].astype(F32)
+    put_rows(w_out, 4 * d + f, f)
+    put_rows(c_proj, rows1, 3 * d)
+    put_rows(c_out, rows1 + 3 * d, d)
+    small = pack[4 * d + 2 * f : 4 * d + 2 * f + 16].astype(F32)
+    bias[...] = small[0:3]
+    for c in range(f // d):
+        b_in[:, c * d : (c + 1) * d] = small[3 + c : 4 + c]
+    b_out[...] = small[7:8]
+    gain[...] = small[8:10]
+    offset[...] = small[10:12]
+    small = pack[rows1 + 4 * d : rows1 + 4 * d + 32].astype(F32)
+    c_bias[...] = small[0:3]
+    c_gain[...] = small[8:9]
+    c_offset[...] = small[10:11]
+    pair[...] = small[16 : 16 + pair.shape[0]]
+
+
+def unpack(pack, rows1, f, pairs):
+    d = pack.shape[1]
+    inside = pl.BlockSpec(memory_space=pltpu.VMEM)
+    shapes = [(3 * d, d), (d, d), (3, d), (d, f), (1, f), (f, d), (1, d), (2, d), (2, d), (3 * d, d), (d, d), (3, d), (1, d), (1, d), (pairs, d)]
+    return pl.pallas_call(
+        functools.partial(unpack_kernel, rows1, f),
+        name="unpack",
+        out_shape=[sds(s, F32) for s in shapes],
+        in_specs=[inside],
+        out_specs=[inside] * len(shapes),
+        compiler_params=pltpu.CompilerParams(vmem_limit_bytes=50 * 2**20),
+    )(pack)
 
 
 def nothing(*refs):
@@ -607,27 +879,28 @@
 
         return lax.cond(section_zero, enc, dec)
 
-    def middle(s, saved, memory):
+    def middle(s, saved, memory, prev):
         def enc():
-            return (saved[1], *blank((nd, F32), (nd, F32), (nd, BF), ((3 * d, d), BF), ((d, d), BF), ((f, d), BF), ((f, d), BF), ((16, d), F32)))
+            return (saved[1], *blank((nd, F32), (nd, F32), (nd, BF), ((2 * f, d), BF), ((4 * d, d), BF), ((16, d), F32)))
 
         def dec():
-            return tuple(dec_mid(mid[s], x[s], pair_rows[s : s + 1], saved[9], memory, cot[s], layer, cross, place))
+            return tuple(dec_mid(mid[s], x[s], pair_rows[s : s + 1], saved[9], memory, cot[s], layer, cross, place, prev))
 
         return lax.cond(section_zero, enc, dec)
 
-    def last(s, saved, done, d_memory):
+    def last(s, saved, done, d_memory, prev, prev_done):
         _, _, q, k, v, mt, lse, ra, na, wide, act, slope, nb, rb = saved
 
         def enc():
-            d_x, dp, do, d1, d2, small = enc_back(src[s], x[s], d_memory, cot[s], layer, place, (q, k, v, mt, lse, na, ra, act, slope, nb, rb))
-            return d_x, dp, do, d1, d2, small
+            before = prev and (prev[3], prev[2], prev[1])
+            return tuple(enc_back(src[s], x[s], d_memory, cot[s], layer, place, (q, k, v, mt, lse, na, ra, act, slope, nb, rb), before))
 
         def dec():
-            d_x, dp, do, small = dec_self_back(tgt[s], na, done[1], done[2], layer, place, (q, k, v, mt, lse, wide, ra))
-            m = done[8]
-            own = jnp.concatenate([small[0:3], m[3:8], small[3:4], m[9:10], small[4:5], m[11:12], small[5:6], jnp.zeros((3, d), F32)])
-            return d_x, dp, do, done[6], done[7], own
+            before = prev and (prev[3], prev[1])
+            d_x, pack_a, small = dec_self_back(
+                tgt[s], na, done[1], done[2], layer, place, (q, k, v, mt, lse, wide, ra), done[6], onehot[s][:, None], before
+            )
+            return d_x, pack_a, done[4], small
 
         return lax.cond(section_zero, enc, dec)
 
@@ -638,32 +911,17 @@
         saved.append(first(s))
         memory.append(lax.ppermute(saved[s][0], "section", ahead))
     for s in range(count):
-        done.append(middle(s, saved[s], memory[s]))
+        done.append(middle(s, saved[s], memory[s], (done[s - 1][6], done[s - 1][4], done[s - 1][5]) if s else ()))
         d_memory.append(lax.ppermute(done[s][3], "section", behind))
     for s in range(count):
-        grads.append(last(s, saved[s], done[s], d_memory[s]))
+        grads.append(last(s, saved[s], done[s], d_memory[s], grads[s - 1] if s else (), done[s - 1] if s else ()))
     shown = jnp.stack([done[s][0] for s in range(count)])
     d_x = jnp.stack([grads[s][0] for s in range(count)])
-
-    def total(parts):
-        return sum(p.astype(F32) for p in parts)
-
-    own = total([g[5] for g in grads])
-    pack = jnp.concatenate([total([g[i] for g in grads]) for i in (1, 2, 3, 4)] + [own]).astype(BF)
-    pair_grad = sum(onehot[s][:, None] * grads[s][5][12:13] for s in range(count))
-    mid_small = total([m[8] for m in done])
-    pack_cross = jnp.concatenate([total([m[4] for m in done]), total([m[5] for m in done]), mid_small, pair_grad]).astype(BF)
-    pack = lax.psum(pack, "dp").astype(F32)
-    pack_cross = lax.psum(jnp.where(section_zero, 0, pack_cross), ("section", "dp")).astype(F32)
-    a, b, c, e = 3 * d, 4 * d, 4 * d + f, 4 * d + 2 * f
-    small = pack[e:]
-    w1 = pack[b:c].reshape(f // d, d, d).transpose(1, 0, 2).reshape(d, f)
-    cs = pack_cross[4 * d :]
+    pack, rows1 = grad_sum(lax.axis_size("dp"), grads[-1][1], grads[-1][2], done[-1][5], grads[-1][3], done[-1][6])
+    proj, out_w, bias, w_in, b_in, w_out, b_out, gain, offset, c_proj, c_out, c_bias, c_gain, c_offset, pair = unpack(pack, rows1, f, pairs)
     return (
-        shown[None], d_x[None],
-        pack[:a].reshape(1, 3, d, d), pack[a:b][None], small[None, 0:3], w1[None], small[3:7].reshape(1, f), pack[c:e][None], small[7:8],
-        small[None, 8:10], small[None, 10:12],
-        pack_cross[:a].reshape(3, d, d), pack_cross[a:b], cs[0:3], cs[8], cs[10], cs[16 : 16 + pairs],
+        shown[None], d_x[None], proj.reshape(1, 3, d, d), out_w[None], bias[None], w_in[None], b_in, w_out[None], b_out, gain[None], offset[None],
+        c_proj.reshape(3, d, d), c_out, c_bias, c_gain[0], c_offset[0], pair,
     )
 
 

time: 660 us -> 451 us (0.68)
  waiting for transfers between devices: 349 us -> 95.4 us
  Pallas kernels: 183 us -> 292 us
  local copies, waits for them, and re-layouts: 48.3 us -> 15.6 us
  other arithmetic: 32.1 us -> 14.7 us
  between operations: 15.4 us -> 1.69 us
    psum x2 -> x0, waiting for transfers between devices: 255 us -> none  [the longest x1 138 us: per_device(): pack = lax.psum(pack, 'dp').astype(F32)]
    pallas_call x0 -> x2, Pallas kernels: none -> 109 us  [the longest x1 99 us: grad_sum(): pl.pallas_call(functools.partial(grad_sum_kernel, count, rows1, rows2), n...]
    slice x11 -> x0, local copies, waits for them, and re-layouts: 12.7 us -> none  [the longest x1 3.66 us: per_device(): pack_cross[:a].reshape(3, d, d)]
    unnamed x4 -> x0, other arithmetic: 8.1 us -> none
  transfers between devices with their start and end apart: 6 -> 4, of which waited for: 5 -> 3; matrix products, arithmetic and copies ran while one was open for 5% -> 3% of each run, Pallas kernels for 14% -> 21%
where the time goes in v2:
time: 451 us; the launch traced here: 442 us
  Pallas kernels  292 us (65%)
  waiting for transfers between devices  95.4 us (21%)
  local copies, waits for them, and re-layouts  15.6 us (3%)
  other arithmetic  14.7 us (3%)
  loops' own time  14.4 us (3%)
  starting transfers between devices  7.17 us (2%)
    pallas_call x4, Pallas kernels, call(): pl.pallas_call(kernel, name=name, out_shape=[sds(*o) for o in outs], in_s...  183 us
    pallas_call x1, Pallas kernels, grad_sum(): pl.pallas_call(functools.partial(grad_sum_kernel, count, rows1, rows2), n...  99 us
    ppermute x2, waiting for transfers between devices, per_device(): d_memory.append(lax.ppermute(done[s][3], 'section', behind))  84.6 us
    another operation x2, loops' own time, middle(): return lax.cond(section_zero, enc, dec)  13 us
    ppermute x2, waiting for transfers between devices, per_device(): memory.append(lax.ppermute(saved[s][0], 'section', ahead))  10.8 us
    pallas_call x1, Pallas kernels, unpack(): pl.pallas_call(functools.partial(unpack_kernel, rows1, f), name='unpack',...  9.76 us
  transfers between devices with their start and end apart: 4, of which 3 were waited for; matrix products, arithmetic and copies ran while one was open for 3% of the time, Pallas kernels for 21%

profile of v2, /device:TPU:1, one launch (start us, length us, event | category | flops | bytes accessed | tf_op | source)
XLA Modules:
  0.0 442.0 jit_solution(5132662481055366177)
XLA Ops:
  0.7 0.0 copy-start
  1.3 1.5 fusion.4
  2.8 0.7 broadcast_select_fusion
  3.5 0.6 fusion.3
  4.1 0.7 copy.43
  4.8 1.4 pad_add_fusion
  6.1 1.4 pad_add_fusion.1
  7.5 0.8 fusion.1
  8.4 0.0 copy-done.39
  8.4 42.7 %conditional.6 = (bf16[1024,512]{1,0:T(8,128)(2,1)}, bf16[1024,512]{1,0:T(8,128)(2,1)S(1)}, bf16[1024,512]{1,0:T(8,128)(2,1)}, bf16[1024,512]{1,0:T(8,128)(2,1)}...) conditional(s32[]{:T(128)} %convert_element_type.4, ...), branch_computations={%region_0.1_spmd, %region_1.2_spmd} | conditional | flops 15000000512 | bytes 25239804 | solution.py:880
  8.4 0.0 copy-start.11
  8.4 0.0 copy-start.18
  8.4 0.0 copy-start.25
  8.4 0.0 copy-start.30
  8.4 2.3 slice_bitcast_fusion.1.x
  10.7 0.0 copy-done.25
  10.8 0.0 copy-done.30
  10.8 40.3 %encoder_forward.2 = (bf16[1024,512]{1,0:T(8,128)(2,1)}, bf16[1024,512]{1,0:T(8,128)(2,1)S(1)}, bf16[1024,512]{1,0:T(8,128)(2,1)}, bf16[1024,512]{1,0:T(8,128)(2...) custom-call(s32[2]{0:T(128)S(1)} %get-tuple-element.378.length, ...), custom_call_target="tpu_custom_call" | custom-call | flops 15000000512 | bytes 20971520 | tf_op jit(solution)/shard_map/cond/branch_1_fun/encoder_forward/pallas_call | solution.py:542
  51.1 2.3 collective-permute-start
  53.4 1.9 pad_add_fusion.2
  55.3 1.3 pad_add_fusion.3
  56.6 0.0 copy-start.35
  56.6 0.0 copy-start.38
  56.6 0.5 copy-done.41
  57.1 43.0 %conditional.8 = (bf16[1024,512]{1,0:T(8,128)(2,1)}, bf16[1024,512]{1,0:T(8,128)(2,1)}, bf16[1024,512]{1,0:T(8,128)(2,1)}, bf16[1024,512]{1,0:T(8,128)(2,1)}, bf...) conditional(s32[]{:T(128)} %convert_element_type.4, ...), branch_computations={%region_4.5_spmd, %region_5.6_spmd} | conditional | flops 15000000512 | bytes 23142624 | solution.py:880
  57.4 0.0 copy-start.12
  57.4 0.0 copy-start.20
  57.4 0.0 copy-start.27
  57.4 0.0 copy-start.31
  57.4 2.3 slice_bitcast_fusion.5.x
  59.8 0.0 copy-done.27
  59.8 40.3 %encoder_forward.3 = (bf16[1024,512]{1,0:T(8,128)(2,1)}, bf16[1024,512]{1,0:T(8,128)(2,1)}, bf16[1024,512]{1,0:T(8,128)(2,1)}, bf16[1024,512]{1,0:T(8,128)(2,1)}...) custom-call(s32[2]{0:T(128)S(1)} %get-tuple-element.455.length, ...), custom_call_target="tpu_custom_call" | custom-call | flops 15000000512 | bytes 20971520 | tf_op jit(solution)/shard_map/cond/branch_1_fun/encoder_forward/pallas_call | solution.py:542
  100.1 2.3 collective-permute-start.1
  102.4 1.4 pad_add_fusion.4
  103.8 0.0 collective-permute-done
  103.8 0.0 copy-done.6
  103.8 7.1 %conditional.7 = (f32[1024,512]{1,0:T(8,128)}, f32[1024,512]{1,0:T(8,128)}, bf16[1024,512]{1,0:T(8,128)(2,1)}, bf16[4096,512]{1,0:T(8,128)(2,1)}, bf16[2048,512]...) conditional(s32[]{:T(128)} %convert_element_type.4, (bf16[2,1024,512]{2,1,0:T(8,128)(2,1)}, ...), branch_computations={%region_2.3_spmd, %region_3.4_spmd} | conditional | flops 54999998464 | bytes 25243816 | solution.py:889
  111.0 1.3 collective-permute-start.2
  112.3 1.3 pad_add_fusion.5
  113.6 10.8 %collective-permute-done.1 = bf16[1024,512]{1,0:T(8,128)(2,1)} collective-permute-done((bf16[1024,512]{1,0:T(8,128)(2,1)}, bf16[1024,512]{1,0:T(8,128)(2,1)}, u32[]{:S(2)}, u32[]{:S(2)}) %collective-permute-start.1) | collective-permute-done | bytes 1048608 | tf_op jit(solution)/shard_map/ppermute | solution.py:912
  124.4 5.8 %conditional.9 = (f32[1024,512]{1,0:T(8,128)}, f32[1024,512]{1,0:T(8,128)}, bf16[1024,512]{1,0:T(8,128)(2,1)}, bf16[4096,512]{1,0:T(8,128)(2,1)}, bf16[2048,512]...) conditional(s32[]{:T(128)} %convert_element_type.4, (bf16[2,1024,512]{2,1,0:T(8,128)(2,1)}, ...), branch_computations={%region_6.7_spmd, %region_7.8_spmd} | conditional | flops 54999998464 | bytes 25243816 | solution.py:889
  130.3 1.3 collective-permute-start.3
  131.6 0.0 copy-done.36
  131.6 0.1 fusion
  131.7 2.8 maximum_bitcast_fusion.1
  134.5 51.9 %collective-permute-done.2 = bf16[1024,512]{1,0:T(8,128)(2,1)} collective-permute-done((bf16[1024,512]{1,0:T(8,128)(2,1)}, bf16[1024,512]{1,0:T(8,128)(2,1)}, u32[]{:S(2)}, u32[]{:S(2)}) %collective-permute-start.2) | collective-permute-done | bytes 1048608 | tf_op jit(solution)/shard_map/ppermute | solution.py:915
  186.4 0.0 copy-done.7
  186.4 0.0 copy-start.37
  186.4 0.0 copy-start.42
  186.4 55.5 %conditional.10 = ((f32[1024,512]{1,0:T(8,128)}, bf16[2048,512]{1,0:T(8,128)(2,1)}, bf16[4096,512]{1,0:T(8,128)(2,1)}, f32[32,512]{1,0:T(8,128)S(1)})) conditional(s32[]{:T(128)} %convert_element_type.4, (f32[2,16]{1,0:T(2,128)S(1)}, s32[2]{0:T(128)S(1)}, bf16[1024,512]{1,0:T(8,128)(2,1)}, f32[1024,512]{1,0:T(8,128)}, f32[1024,512]{1,0:T(8,128)}, ...), branch_computations={%region_8.9_spmd, %region_9.10_spmd} | conditional | flops 35000000512 | bytes 33554496 | solution.py:905
  186.6 0.8 copy-done.10
  187.4 3.1 slice_bitcast_fusion.9
  190.5 51.2 %encoder_back.2 = (f32[1024,512]{1,0:T(8,128)}, bf16[2048,512]{1,0:T(8,128)(2,1)}, bf16[4096,512]{1,0:T(8,128)(2,1)}, f32[32,512]{1,0:T(8,128)S(1)}) custom-call(s32[2]{0:T(128)S(1)} %get-tuple-element.534.length, bf16[1024,512]{1,0:T(8,128)(2,1)} %get-tuple-element.773.x, bf16[1024,512]{1,0:T(8,128)(2,1)} %get-tuple-element.536.d_memory, ...), custom_call_target="tpu_custom_call" | custom-call | flops 35000000512 | bytes 20971520 | tf_op jit(solution)/shard_map/cond/branch_1_fun/encoder_back/pallas_call | solution.py:542
  241.9 32.7 %collective-permute-done.3 = bf16[1024,512]{1,0:T(8,128)(2,1)} collective-permute-done((bf16[1024,512]{1,0:T(8,128)(2,1)}, bf16[1024,512]{1,0:T(8,128)(2,1)}, u32[]{:S(2)}, u32[]{:S(2)}) %collective-permute-start.3) | collective-permute-done | bytes 1048608 | tf_op jit(solution)/shard_map/ppermute | solution.py:915
  274.6 55.3 %conditional.11 = ((f32[1024,512]{1,0:T(8,128)}, bf16[2048,512]{1,0:T(8,128)(2,1)}, bf16[4096,512]{1,0:T(8,128)(2,1)}, f32[32,512]{1,0:T(8,128)S(1)})) conditional(s32[]{:T(128)} %convert_element_type.4, (f32[2,16]{1,0:T(2,128)S(1)}, s32[2]{0:T(128)}, bf16[1024,512]{1,0:T(8,128)(2,1)}, f32[1024,512]{1,0:T(8,128)}, f32[1024,512]{1,0:T(8,128)}, ...), branch_computations={%region_10.11_spmd, %region_11.12_spmd} | conditional | flops 35000000512 | bytes 31457316 | solution.py:905
  275.0 0.0 copy-start.5
  275.0 3.1 slice_bitcast_fusion.12
  278.1 51.6 %encoder_back.3 = (f32[1024,512]{1,0:T(8,128)}, bf16[2048,512]{1,0:T(8,128)(2,1)}, bf16[4096,512]{1,0:T(8,128)(2,1)}, f32[32,512]{1,0:T(8,128)S(1)}) custom-call(s32[2]{0:T(128)S(1)} %get-tuple-element.579.length, bf16[1024,512]{1,0:T(8,128)(2,1)} %get-tuple-element.775.x, bf16[1024,512]{1,0:T(8,128)(2,1)} %get-tuple-element.581.d_memory, ...), custom_call_target="tpu_custom_call" | custom-call | flops 35000000512 | bytes 20971520 | tf_op jit(solution)/shard_map/cond/branch_1_fun/encoder_back/pallas_call | solution.py:542
  330.0 99.0 %gradient_sum.1.pack = bf16[8704,512]{1,0:T(8,128)(2,1)} custom-call(bf16[2048,512]{1,0:T(8,128)(2,1)} %get-tuple-element.732.a, bf16[4096,512]{1,0:T(8,128)(2,1)} %get-tuple-element.733.b, bf16[2048,512]{1,0:T(8,128)(2,1)} %get-tuple-element.734.c, f32[32,512]{1,0:T(8,128)S(1)} %get-tuple-element.735.own, f32[16,512]{1,0:T(8,128)S(1)} %get-tuple-element.721.mids), custom_call_target="tpu_custom_call" | custom-call | tf_op jit(solution)/shard_map/gradient_sum/pallas_call | solution.py:777
  429.0 0.0 copy-start.2
  429.0 0.0 copy-start.3
  429.0 9.8 %unpack.1 = (f32[1536,512]{1,0:T(8,128)}, f32[512,512]{1,0:T(8,128)}, f32[3,512]{1,0:T(4,128)S(1)}, f32[512,2048]{1,0:T(8,128)}, f32[1,2048]{1,0:T(1,128)}, /*in...) custom-call(bf16[8704,512]{1,0:T(8,128)(2,1)} %gradient_sum.1.pack), custom_call_target="tpu_custom_call" | custom-call | tf_op jit(solution)/shard_map/unpack/pallas_call | solution.py:828
  438.8 0.6 copy.40
  439.4 2.5 maximum_bitcast_fusion
  (40 shorter events, 0.1 us)
Async XLA Ops:
  0.7 6.9 %copy-start = (f32[16,512]{1,0:T(8,128)S(1)}, f32[16,512]{1,0:T(8,128)}, u32[]{:S(2)}) copy-start(f32[16,512]{1,0:T(8,128)} %param.52) | copy-start | bytes 98308
  7.5 0.9 copy-start.39
  8.4 2.4 copy-start.9
  8.4 2.4 copy-start.11
  8.4 2.4 copy-start.18
  8.4 2.4 copy-start.25
  8.4 2.3 copy-start.30
  51.1 52.7 %collective-permute-start = (bf16[1024,512]{1,0:T(8,128)(2,1)}, bf16[1024,512]{1,0:T(8,128)(2,1)}, u32[]{:S(2)}, u32[]{:S(2)}) collective-permute-start(bf16[1024,512]{1,0:T(8,128)(2,1)} %get-tuple-element.687), channel_id=1, source_target_pairs={{0,16},{1,17},{2,18},{3,19},{4,20},{5,21},{6,22},{7,23},{8,24},{9,... | collective-permute-start | bytes 3145736 | tf_op jit(solution)/shard_map/ppermute | solution.py:912
  56.6 0.5 copy-start.41
  56.6 47.2 %copy-start.6 = (bf16[512,512]{1,0:T(8,128)(2,1)S(1)}, bf16[512,512]{1,0:T(8,128)(2,1)}, u32[]{:S(2)}) copy-start(bf16[512,512]{1,0:T(8,128)(2,1)} %param.48) | copy-start | bytes 1572868
  56.6 47.2 %copy-start.15 = (f32[3,512]{1,0:T(4,128)S(1)}, f32[3,512]{1,0:T(4,128)}, u32[]{:S(2)}) copy-start(f32[3,512]{1,0:T(4,128)} %param.49) | copy-start | bytes 18436
  56.6 47.2 %copy-start.34 = (f32[512]{0:T(512)S(1)}, f32[512]{0:T(512)}, u32[]{:S(2)}) copy-start(f32[512]{0:T(512)} %param.50) | copy-start | bytes 6148
  56.6 47.2 %copy-start.35 = (f32[512]{0:T(512)S(1)}, f32[512]{0:T(512)}, u32[]{:S(2)}) copy-start(f32[512]{0:T(512)} %param.51) | copy-start | bytes 6148
  56.6 47.2 %copy-start.38 = (bf16[16,512]{1,0:T(8,128)(2,1)S(1)}, bf16[16,512]{1,0:T(8,128)(2,1)}, u32[]{:S(2)}) copy-start(bf16[16,512]{1,0:T(8,128)(2,1)} %constant.10.clone) | copy-start | bytes 49156
  57.4 2.4 copy-start.12
  57.4 2.4 copy-start.20
  57.4 2.3 copy-start.27
  57.4 2.3 copy-start.31
  100.1 24.3 %collective-permute-start.1 = (bf16[1024,512]{1,0:T(8,128)(2,1)}, bf16[1024,512]{1,0:T(8,128)(2,1)}, u32[]{:S(2)}, u32[]{:S(2)}) collective-permute-start(bf16[1024,512]{1,0:T(8,128)(2,1)} %get-tuple-element.691), channel_id=1, source_target_pairs={{0,16},{1,17},{2,18},{3,19},{4,20},{5,21},{6,22},{7,23},{8,24},{9,... | collective-permute-start | bytes 3145736 | tf_op jit(solution)/shard_map/ppermute | solution.py:912
  111.0 75.4 %collective-permute-start.2 = (bf16[1024,512]{1,0:T(8,128)(2,1)}, bf16[1024,512]{1,0:T(8,128)(2,1)}, u32[]{:S(2)}, u32[]{:S(2)}) collective-permute-start(bf16[1024,512]{1,0:T(8,128)(2,1)} %get-tuple-element.706), channel_id=1, source_target_pairs={{16,0},{17,1},{18,2},{19,3},{20,4},{21,5},{22,6},{23,7},{24,8},{25... | collective-permute-start | bytes 3145736 | tf_op jit(solution)/shard_map/ppermute | solution.py:915
  124.4 7.2 %copy-start.36 = (s32[2]{0:T(128)S(1)}, s32[2]{0:T(128)}, u32[]{:S(2)}) copy-start(s32[2]{0:T(128)} %param.35) | copy-start | bytes 28
  130.3 144.3 %collective-permute-start.3 = (bf16[1024,512]{1,0:T(8,128)(2,1)}, bf16[1024,512]{1,0:T(8,128)(2,1)}, u32[]{:S(2)}, u32[]{:S(2)}) collective-permute-start(bf16[1024,512]{1,0:T(8,128)(2,1)} %get-tuple-element.725), channel_id=1, source_target_pairs={{16,0},{17,1},{18,2},{19,3},{20,4},{21,5},{22,6},{23,7},{24,8},{25... | collective-permute-start | bytes 3145736 | tf_op jit(solution)/shard_map/ppermute | solution.py:915
  131.7 54.7 %copy-start.7 = (bf16[1,512,512]{2,1,0:T(8,128)(2,1)S(1)}, bf16[1,512,512]{2,1,0:T(8,128)(2,1)}, u32[]{:S(2)}) copy-start(bf16[1,512,512]{2,1,0:T(8,128)(2,1)} %param.39) | copy-start | bytes 1572868
  131.7 54.7 %copy-start.16 = (f32[1,2,512]{2,1,0:T(2,128)S(1)}, f32[1,2,512]{2,1,0:T(2,128)}, u32[]{:S(2)}) copy-start(f32[1,2,512]{2,1,0:T(2,128)} %param.45) | copy-start | bytes 12292
  131.7 54.7 %copy-start.23 = (f32[1,2,512]{2,1,0:T(2,128)S(1)}, f32[1,2,512]{2,1,0:T(2,128)}, u32[]{:S(2)}) copy-start(f32[1,2,512]{2,1,0:T(2,128)} %param.46) | copy-start | bytes 12292
  131.7 54.7 %copy-start.40 = (s32[2]{0:T(128)S(1)}, s32[2]{0:T(128)}, u32[]{:S(2)}) copy-start(s32[2]{0:T(128)} %copy-done.39) | copy-start | bytes 28
  186.4 88.2 %copy-start.37 = (f32[8,1,1024]{2,1,0:T(1,128)S(1)}, f32[8,1,1024]{2,1,0:T(1,128)}, u32[]{:S(2)}) copy-start(f32[8,1,1024]{2,1,0:T(1,128)} %get-tuple-element.719) | copy-start | bytes 98308
  186.4 88.2 %copy-start.42 = (s32[2]{0:T(128)S(1)}, s32[2]{0:T(128)}, u32[]{:S(2)}) copy-start(s32[2]{0:T(128)} %copy-done.41) | copy-start | bytes 28
  186.6 0.8 copy-start.10
  187.4 3.1 copy-start.4
  275.0 3.1 copy-start.5
  429.0 10.4 %copy-start.2 = (f32[1024,512]{1,0:T(8,128)S(1)}, f32[1024,512]{1,0:T(8,128)}, u32[]{:S(2)}) copy-start(f32[1024,512]{1,0:T(8,128)} %get-tuple-element.711) | copy-start | bytes 6291460
  429.0 10.4 %copy-start.3 = (f32[1024,512]{1,0:T(8,128)S(1)}, f32[1024,512]{1,0:T(8,128)}, u32[]{:S(2)}) copy-start(f32[1024,512]{1,0:T(8,128)} %get-tuple-element.731) | copy-start | bytes 6291460
  439.4 2.5 copy-start.1
